TPU v7x, 128 devices: a whole 4x4x4 slice. The times are simulated.
128 devices in a mesh: grp: 8 (over z, core), mem: 16 (over y, x).
Axes of the slice: x: 4, y: 4, z: 4, core: 2. Of those that a mesh axis runs over, the one named last changes fastest.
Arguments:
- a_tiles: bfloat16 [6144, 7, 128, 128], P(('grp', 'mem')), may hold values from -0.1875 to 0.1875
- p_tiles: bfloat16 [6144, 3, 128, 128], P(('grp', 'mem')), may hold values from -0.5 to 0.5
- a_offsets: int32 [6144, 7], P(('grp', 'mem')), may hold values from -4 to 4, as said below
- agg_counts: int32 [8, 16], replicated, may hold values from 1 to 12, as said below
- row_counts: int32 [8, 16], replicated, may hold values from 4 to 48, as said below
- flows: int32 [8, 2], replicated, may hold values from 1 to 12, as said below
Outputs:
- coarse_tiles: float32 [944, 7, 128, 128], P('grp', None, 'mem')
Inputs may be any that keep to these rules, and one draw needn't show every extreme that they name: `a_offsets`: each row's 7 offsets are distinct, the first is 0 and the others are nonzero. `agg_counts`: the counts of the 16 devices of each group sum to 96; in every group some device has 12 and some has 1. `row_counts`: each device has between 4 and 8 times its aggregate count of live rows, and at most 48; a device with 12 aggregates has 48 rows. `flows`: both ends are reached in every draw, and some group owns 118 coarse rows.
All inputs are finite; a program needn't handle non-finite values.
Results may differ from a plain program's by a relative error of at most 0.0029.
Values may be sent and summed in bfloat16 or wider, within the bound.
A program may use at most 128 MiB of HBM per device.

v0:
```python
import jax
import jax.numpy as jnp
from jax import lax
from jax.sharding import PartitionSpec as P


def passed_along(shard, axis, by):
    devices = lax.axis_size(axis)
    return lax.ppermute(shard, axis, [(i, (i + by) % devices) for i in range(devices)])


def local(a_tiles, p_tiles, a_offsets, agg_counts, row_counts, flows):
    slot_cap = a_tiles.shape[0]
    tile_size = a_tiles.shape[2]
    group_count = lax.axis_size("grp")
    member_count = lax.axis_size("mem")
    device_total = group_count * member_count
    group_idx = lax.axis_index("grp")
    member_idx = lax.axis_index("mem")
    device_idx = group_idx * member_count + member_idx
    flat_aggs = agg_counts.reshape(-1)
    flat_rows = row_counts.reshape(-1)
    own_aggs = flat_aggs[device_idx]
    own_rows = flat_rows[device_idx]
    prev_rows = flat_rows[(device_idx - 1) % device_total]
    agg_cap = slot_cap // 4
    row_ids = jnp.arange(slot_cap, dtype=jnp.int32)
    row_agg = row_ids * own_aggs // own_rows
    before_rows = passed_along(p_tiles, ("grp", "mem"), 1)
    after_rows = passed_along(p_tiles, ("grp", "mem"), -1)
    after_base = slot_cap + slot_cap
    ghost_table = jnp.concatenate([before_rows, p_tiles, after_rows], 0)
    target = row_ids[:, None] + a_offsets
    table_row = jnp.where(
        target < 0,
        prev_rows + target,
        jnp.where(target < own_rows, slot_cap + target, after_base + target - own_rows),
    )
    table_row = jnp.clip(table_row, 0, ghost_table.shape[0] - 1)
    their_agg = jnp.where(
        target < 0, -1, jnp.where(target < own_rows, target * own_aggs // own_rows, own_aggs)
    )
    live_mask = (row_ids < own_rows).astype(jnp.float32)
    band_slot = (
        (their_agg - row_agg[:, None])[:, :, None]
        + jnp.arange(3, dtype=jnp.int32)[None, None, :]
        + 1
    )
    block_rows = 8

    def accumulate(turn_index, running):
        first_row = turn_index * block_rows
        a_block = lax.dynamic_slice_in_dim(a_tiles, first_row, block_rows, 0)
        rows_block = lax.dynamic_slice_in_dim(table_row, first_row, block_rows, 0)
        gathered = ghost_table[rows_block]
        products = jnp.einsum(
            "rkab,rkqbc->rkqac", a_block, gathered, preferred_element_type=jnp.float32
        )
        slot_block = lax.dynamic_slice_in_dim(band_slot, first_row, block_rows, 0)
        merged = jnp.stack(
            [
                jnp.sum(
                    jnp.where((slot_block == column)[:, :, :, None, None], products, 0.0),
                    axis=(1, 2),
                )
                for column in range(5)
            ],
            1,
        ).astype(jnp.bfloat16)
        p_block = lax.dynamic_slice_in_dim(p_tiles, first_row, block_rows, 0)
        triple = jnp.einsum("rpba,rebc->rpeac", p_block, merged, preferred_element_type=jnp.float32)
        placed = jnp.stack(
            [
                jnp.pad(triple[:, branch], ((0, 0), (2 - branch, branch), (0, 0), (0, 0)))
                for branch in range(3)
            ],
            1,
        )
        agg_block = lax.dynamic_slice_in_dim(row_agg, first_row, block_rows, 0)
        live_block = lax.dynamic_slice_in_dim(live_mask, first_row, block_rows, 0)
        for line in range(block_rows):
            weighted = placed[line] * live_block[line]
            current = lax.dynamic_slice_in_dim(running, agg_block[line], 3, 0)
            running = lax.dynamic_update_slice_in_dim(
                running, current + weighted, agg_block[line], 0
            )
        return running

    partial_rows = lax.fori_loop(
        0,
        slot_cap // block_rows,
        accumulate,
        jnp.zeros((agg_cap + 2, 7, tile_size, tile_size), jnp.float32),
    )
    from_after = passed_along(partial_rows[0], ("grp", "mem"), -1)
    spill_row = lax.dynamic_index_in_dim(partial_rows, own_aggs + 1, 0, keepdims=False)
    from_before = passed_along(spill_row, ("grp", "mem"), 1)
    local_ids = jnp.arange(agg_cap, dtype=jnp.int32)
    complete = partial_rows[1 : agg_cap + 1]
    complete = (
        complete
        + (local_ids == own_aggs - 1).astype(jnp.float32)[:, None, None, None] * from_after[None]
    )
    complete = (
        complete + (local_ids == 0).astype(jnp.float32)[:, None, None, None] * from_before[None]
    )
    complete = complete * (local_ids < own_aggs).astype(jnp.float32)[:, None, None, None]
    share_rows = tile_size // member_count
    pieces = complete.reshape(agg_cap, 7, member_count, share_rows, tile_size)
    received = lax.all_to_all(pieces, "mem", split_axis=2, concat_axis=0, tiled=True)
    group_aggs = agg_counts[group_idx]
    member_ends = jnp.cumsum(group_aggs)
    begins = member_ends - group_aggs
    group_rows = member_count * agg_cap // 2
    position = jnp.arange(group_rows, dtype=jnp.int32)
    owner_member = jnp.sum((position[:, None] >= member_ends[None, :]).astype(jnp.int32), axis=1)
    source = owner_member * agg_cap + position - begins[owner_member]
    native = received[source].reshape(group_rows, 7, share_rows, tile_size)
    flow_cap = group_rows // 8
    from_lower = passed_along(native[group_rows - flow_cap :], "grp", 1)
    from_upper = passed_along(native[:flow_cap], "grp", -1)
    out_cap = group_rows + 2 * flow_cap - 2
    extended = jnp.concatenate([from_lower, native, from_upper], 0)
    give_forward = flows[group_idx, 0]
    give_back = flows[group_idx, 1]
    take_lower = flows[(group_idx - 1) % group_count, 0]
    take_upper = flows[(group_idx + 1) % group_count, 1]
    middle = group_rows - give_forward - give_back
    slot_ids = jnp.arange(out_cap, dtype=jnp.int32)
    picked = jnp.where(
        slot_ids < take_lower,
        flow_cap - take_lower + slot_ids,
        jnp.where(
            slot_ids < take_lower + middle,
            flow_cap + give_back + slot_ids - take_lower,
            flow_cap + group_rows + slot_ids - take_lower - middle,
        ),
    )
    picked = jnp.clip(picked, 0, extended.shape[0] - 1)
    keep_mask = (slot_ids < take_lower + middle + take_upper).astype(jnp.float32)
    return extended[picked] * keep_mask[:, None, None, None]


def solution(mesh):
    placed = (
        P(("grp", "mem"), None, None, None),
        P(("grp", "mem"), None, None, None),
        P(("grp", "mem"), None),
        P(),
        P(),
        P(),
    )
    return jax.shard_map(
        local, mesh=mesh, in_specs=placed, out_specs=P("grp", None, "mem", None), check_vma=False
    )
```

profile of v0, /device:TPU:1, one launch (start us, length us, event | category | flops | bytes accessed | tf_op | source)
XLA Modules:
  0.0 728.4 jit_solution(18199672043651721353)
XLA Ops:
  2.0 4.3 collective-permute-start.1
  16.1 92.2 %collective-permute-done = bf16[48,3,128,128]{3,2,1,0:T(8,128)(2,1)} collective-permute-done((bf16[48,3,128,128]{3,2,1,0:T(8,128)(2,1)}, bf16[48,3,128,128]{3,2,1,0:T(8,128)(2,1)}, u32[]{:S(2)}, u32[]{:S(2)}) %collective-permute-start) | collective-permute-done | bytes 4718624 | tf_op jit(solution)/shard_map/ppermute | solution.py:9
  108.4 12.6 %pad_maximum_fusion.1 = bf16[144,3,128,128]{3,2,1,0:T(8,128)(2,1)} fusion(bf16[48,3,128,128]{3,2,1,0:T(8,128)(2,1)} %collective-permute-done.1, bf16[48,3,128,128]{3,2,1,0:T(8,128)(2,1)} %param.9, bf16[48,3,128,128]{3,2,1,0:T(8,128)(2,1)} %collective-permute-done), kind=kLoop, calls=%fused_computation.76 | loop fusion | flops 14155776 | bytes 28311552 | tf_op jit(solution)/shard_map/concatenate | solution.py:32
  124.6 462.8 %while.15 = (s32[]{:T(128)}, f32[14,7,128,128]{2,3,1,0:T(8,128)}, s32[48]{0:T(128)S(1)}, s32[48,7,3]{2,1,0:T(8,128)S(1)}, s32[48,7]{1,0:T(8,128)S(1)}, /*index=5...) while((s32[]{:T(128)}, f32[14,7,128,128]{2,3,1,0:T(8,128)}, ...), condition=%wide.region_6.7_spmd, body=%wide.region_0.6_spmd.sunk | while | flops 1245841408 | bytes 121911152 | solution.py:89
  125.3 8.7 %gather_fusion = bf16[56,3,128,128]{3,2,1,0:T(8,128)(2,1)} fusion(bf16[144,3,128,128]{3,2,1,0:T(8,128)(2,1)} %get-tuple-element.453, s32[1024]{0:T(1024)S(1)} %pad_clamp_fusion.4), kind=kCustom, calls=%fused_computation.clone.1 | custom fusion | bytes 11010272 | tf_op jit(solution)/shard_map/while/body/eval_jaxpr/gather | solution.py:55
  134.0 9.4 %select_reduce_fusion.6 = (bf16[8,128,128]{2,1,0:T(8,128)(2,1)S(1)}, bf16[8,128,128]{2,1,0:T(8,128)(2,1)S(1)}, bf16[8,128,128]{2,1,0:T(8,128)(2,1)S(1)}, bf16[8,...) fusion(pred[8,7,3]{2,1,0:T(8,128)(4,1)S(1)} %get-tuple-element.390, ...), kind=kOutput, calls=%fused_computation.4.clone.1 | convolution fusion | flops 731512832 | bytes 8651596 | tf_op jit(solution)/shard_map/while/body/eval_jaxpr/rkab,rkqbc->rkqac/dot_general | solution.py:56
  148.1 5.8 pad_maximum_fusion.4
  158.2 3.8 fusion.80
  163.8 3.8 fusion.81
  169.6 3.8 fusion.82
  175.5 3.7 fusion.83
  181.0 3.8 fusion.84
  186.8 3.8 fusion.85
  198.4 3.8 fusion.87
  202.9 8.7 %gather_fusion = bf16[56,3,128,128]{3,2,1,0:T(8,128)(2,1)} fusion(bf16[144,3,128,128]{3,2,1,0:T(8,128)(2,1)} %get-tuple-element.453, s32[1024]{0:T(1024)S(1)} %pad_clamp_fusion.4), kind=kCustom, calls=%fused_computation.clone.1 | custom fusion | bytes 11010272 | tf_op jit(solution)/shard_map/while/body/eval_jaxpr/gather | solution.py:55
  211.7 9.4 %select_reduce_fusion.6 = (bf16[8,128,128]{2,1,0:T(8,128)(2,1)S(1)}, bf16[8,128,128]{2,1,0:T(8,128)(2,1)S(1)}, bf16[8,128,128]{2,1,0:T(8,128)(2,1)S(1)}, bf16[8,...) fusion(pred[8,7,3]{2,1,0:T(8,128)(4,1)S(1)} %get-tuple-element.390, ...), kind=kOutput, calls=%fused_computation.4.clone.1 | convolution fusion | flops 731512832 | bytes 8651596 | tf_op jit(solution)/shard_map/while/body/eval_jaxpr/rkab,rkqbc->rkqac/dot_general | solution.py:56
  225.8 5.8 pad_maximum_fusion.4
  235.9 3.7 fusion.80
  241.5 3.8 fusion.81
  247.2 3.7 fusion.82
  258.4 3.7 fusion.84
  264.1 3.7 fusion.85
  275.5 3.7 fusion.87
  280.0 8.7 %gather_fusion = bf16[56,3,128,128]{3,2,1,0:T(8,128)(2,1)} fusion(bf16[144,3,128,128]{3,2,1,0:T(8,128)(2,1)} %get-tuple-element.453, s32[1024]{0:T(1024)S(1)} %pad_clamp_fusion.4), kind=kCustom, calls=%fused_computation.clone.1 | custom fusion | bytes 11010272 | tf_op jit(solution)/shard_map/while/body/eval_jaxpr/gather | solution.py:55
  288.7 9.4 %select_reduce_fusion.6 = (bf16[8,128,128]{2,1,0:T(8,128)(2,1)S(1)}, bf16[8,128,128]{2,1,0:T(8,128)(2,1)S(1)}, bf16[8,128,128]{2,1,0:T(8,128)(2,1)S(1)}, bf16[8,...) fusion(pred[8,7,3]{2,1,0:T(8,128)(4,1)S(1)} %get-tuple-element.390, ...), kind=kOutput, calls=%fused_computation.4.clone.1 | convolution fusion | flops 731512832 | bytes 8651596 | tf_op jit(solution)/shard_map/while/body/eval_jaxpr/rkab,rkqbc->rkqac/dot_general | solution.py:56
  302.8 5.8 pad_maximum_fusion.4
  312.9 3.7 fusion.80
  318.4 3.7 fusion.81
  324.1 3.7 fusion.82
  335.3 3.7 fusion.84
  341.0 3.7 fusion.85
  352.5 3.7 fusion.87
  356.9 8.7 %gather_fusion = bf16[56,3,128,128]{3,2,1,0:T(8,128)(2,1)} fusion(bf16[144,3,128,128]{3,2,1,0:T(8,128)(2,1)} %get-tuple-element.453, s32[1024]{0:T(1024)S(1)} %pad_clamp_fusion.4), kind=kCustom, calls=%fused_computation.clone.1 | custom fusion | bytes 11010272 | tf_op jit(solution)/shard_map/while/body/eval_jaxpr/gather | solution.py:55
  365.6 9.4 %select_reduce_fusion.6 = (bf16[8,128,128]{2,1,0:T(8,128)(2,1)S(1)}, bf16[8,128,128]{2,1,0:T(8,128)(2,1)S(1)}, bf16[8,128,128]{2,1,0:T(8,128)(2,1)S(1)}, bf16[8,...) fusion(pred[8,7,3]{2,1,0:T(8,128)(4,1)S(1)} %get-tuple-element.390, ...), kind=kOutput, calls=%fused_computation.4.clone.1 | convolution fusion | flops 731512832 | bytes 8651596 | tf_op jit(solution)/shard_map/while/body/eval_jaxpr/rkab,rkqbc->rkqac/dot_general | solution.py:56
  379.8 5.8 pad_maximum_fusion.4
  389.8 3.7 fusion.80
  395.4 3.7 fusion.81
  401.0 3.7 fusion.82
  412.2 3.7 fusion.84
  417.9 3.7 fusion.85
  429.4 3.7 fusion.87
  433.8 8.7 %gather_fusion = bf16[56,3,128,128]{3,2,1,0:T(8,128)(2,1)} fusion(bf16[144,3,128,128]{3,2,1,0:T(8,128)(2,1)} %get-tuple-element.453, s32[1024]{0:T(1024)S(1)} %pad_clamp_fusion.4), kind=kCustom, calls=%fused_computation.clone.1 | custom fusion | bytes 11010272 | tf_op jit(solution)/shard_map/while/body/eval_jaxpr/gather | solution.py:55
  442.5 9.4 %select_reduce_fusion.6 = (bf16[8,128,128]{2,1,0:T(8,128)(2,1)S(1)}, bf16[8,128,128]{2,1,0:T(8,128)(2,1)S(1)}, bf16[8,128,128]{2,1,0:T(8,128)(2,1)S(1)}, bf16[8,...) fusion(pred[8,7,3]{2,1,0:T(8,128)(4,1)S(1)} %get-tuple-element.390, ...), kind=kOutput, calls=%fused_computation.4.clone.1 | convolution fusion | flops 731512832 | bytes 8651596 | tf_op jit(solution)/shard_map/while/body/eval_jaxpr/rkab,rkqbc->rkqac/dot_general | solution.py:56
  456.7 5.8 pad_maximum_fusion.4
  472.3 3.7 fusion.81
  489.1 3.7 fusion.84
  494.7 3.7 fusion.85
  506.2 3.8 fusion.87
  510.7 8.7 %gather_fusion = bf16[56,3,128,128]{3,2,1,0:T(8,128)(2,1)} fusion(bf16[144,3,128,128]{3,2,1,0:T(8,128)(2,1)} %get-tuple-element.453, s32[1024]{0:T(1024)S(1)} %pad_clamp_fusion.4), kind=kCustom, calls=%fused_computation.clone.1 | custom fusion | bytes 11010272 | tf_op jit(solution)/shard_map/while/body/eval_jaxpr/gather | solution.py:55
  519.4 9.4 %select_reduce_fusion.6 = (bf16[8,128,128]{2,1,0:T(8,128)(2,1)S(1)}, bf16[8,128,128]{2,1,0:T(8,128)(2,1)S(1)}, bf16[8,128,128]{2,1,0:T(8,128)(2,1)S(1)}, bf16[8,...) fusion(pred[8,7,3]{2,1,0:T(8,128)(4,1)S(1)} %get-tuple-element.390, ...), kind=kOutput, calls=%fused_computation.4.clone.1 | convolution fusion | flops 731512832 | bytes 8651596 | tf_op jit(solution)/shard_map/while/body/eval_jaxpr/rkab,rkqbc->rkqac/dot_general | solution.py:56
  533.6 5.8 pad_maximum_fusion.4
  543.7 3.7 fusion.80
  549.2 3.8 fusion.81
  554.9 3.7 fusion.82
  566.2 3.8 fusion.84
  571.9 3.8 fusion.85
  583.5 3.8 fusion.87
  587.3 7.8 %copy.77 = f32[14,7,128,128]{3,2,1,0:T(8,128)} copy(f32[14,7,128,128]{2,3,1,0:T(8,128)} %get-tuple-element.225) | data formatting | bytes 12845056 | tf_op jit(solution)/shard_map/while | solution.py:89
  600.8 4.2 collective-permute-done.2
  605.2 5.6 collective-permute-done.3
  617.4 8.1 %all-to-all-start = ((f32[12,7,16,8,128]{4,3,1,0,2:T(8,128)}), f32[12,7,16,8,128]{4,3,1,0,2:T(8,128)}, u32[]{:S(2)}, u32[]{:S(2)}) async-start(f32[12,7,16,8,128]{4,3,1,0,2:T(8,128)} %copy.80), calls=%async_computation | async-start | bytes 11010048 | tf_op jit(solution)/shard_map/all_to_all | solution.py:110
  627.9 10.0 %fusion.52 = s32[96]{0:T(128)S(1)} fusion(s32[96]{0:T(128)S(1)} %convert_reduce_fusion, s32[]{:T(128)} %bitcast.78, s32[]{:T(128)} %bitcast.79, s32[]{:T(128)} %bitcast.80, s32[]{:T(128)} %bitcast.81, s32[]{:T(128)} %bitcast.82, s32[]{:T(128)} %bitcast.84, s32[]{:T(128)} %bitcast.83, s32[]{:T(128)} %bitcast.61, s32[]{:T(128)} %bitcast.63, s32[]{:T(128)} %bitcast.65, ...), kind=kLoop, calls=%fused_computation.134 | loop fusion | flops 3744 | bytes 832 | tf_op jit(solution)/shard_map/select_n | solution.py:118
  637.9 50.8 %all-to-all-done = f32[12,7,16,8,128]{4,3,1,0,2:T(8,128)} async-done(((f32[12,7,16,8,128]{4,3,1,0,2:T(8,128)}), f32[12,7,16,8,128]{4,3,1,0,2:T(8,128)}, u32[]{:S(2)}, u32[]{:S(2)}) %all-to-all-start) | async-done | bytes 5505056 | tf_op jit(solution)/shard_map/all_to_all | solution.py:110
  692.0 21.9 %collective-permute-start.4 = (f32[12,7,8,128]{3,2,1,0:T(8,128)S(1)}, f32[12,7,8,128]{3,2,1,0:T(8,128)}, u32[]{:S(2)}, u32[]{:S(2)}) collective-permute-start(f32[12,7,8,128]{3,2,1,0:T(8,128)S(1)} %get-tuple-element.275), channel_id=1, source_target_pairs={{0,16},{16,32},{32,48},{48,64},{64,80},{80,96},{96,112},{112,0},{1... | collective-permute-start | bytes 1032200 | tf_op jit(solution)/shard_map/ppermute | solution.py:9
  (182 shorter events, 134.4 us)
Async XLA Ops:
  0.0 108.4 %collective-permute-start = (bf16[48,3,128,128]{3,2,1,0:T(8,128)(2,1)}, bf16[48,3,128,128]{3,2,1,0:T(8,128)(2,1)}, u32[]{:S(2)}, u32[]{:S(2)}) collective-permute-start(bf16[48,3,128,128]{3,2,1,0:T(8,128)(2,1)} %param.9), channel_id=1, source_target_pairs={{0,1},{1,2},{2,3},{3,4},{4,5},{5,6},{6,7},{7,8},{8,9},{9,10},{10,1... | collective-permute-start | bytes 14155784 | tf_op jit(solution)/shard_map/ppermute | solution.py:9
  2.0 106.4 %collective-permute-start.1 = (bf16[48,3,128,128]{3,2,1,0:T(8,128)(2,1)}, bf16[48,3,128,128]{3,2,1,0:T(8,128)(2,1)}, u32[]{:S(2)}, u32[]{:S(2)}) collective-permute-start(bf16[48,3,128,128]{3,2,1,0:T(8,128)(2,1)} %param.9), channel_id=1, source_target_pairs={{0,127},{1,0},{2,1},{3,2},{4,3},{5,4},{6,5},{7,6},{8,7},{9,8},{10,... | collective-permute-start | bytes 14155784 | tf_op jit(solution)/shard_map/ppermute | solution.py:9
  124.6 0.6 copy-start.1
  192.7 9.5 %copy-start.2 = (s32[48]{0:T(128)S(1)}, s32[48]{0:T(128)}, u32[]{:S(2)}) copy-start(s32[48]{0:T(128)} %copy-done.1) | copy-start | bytes 580 | tf_op jit(solution)/shard_map/while
  202.2 0.6 copy-start.1
  269.8 9.4 %copy-start.2 = (s32[48]{0:T(128)S(1)}, s32[48]{0:T(128)}, u32[]{:S(2)}) copy-start(s32[48]{0:T(128)} %copy-done.1) | copy-start | bytes 580 | tf_op jit(solution)/shard_map/while
  279.2 0.6 copy-start.1
  346.8 9.4 %copy-start.2 = (s32[48]{0:T(128)S(1)}, s32[48]{0:T(128)}, u32[]{:S(2)}) copy-start(s32[48]{0:T(128)} %copy-done.1) | copy-start | bytes 580 | tf_op jit(solution)/shard_map/while
  356.2 0.6 copy-start.1
  423.7 9.4 %copy-start.2 = (s32[48]{0:T(128)S(1)}, s32[48]{0:T(128)}, u32[]{:S(2)}) copy-start(s32[48]{0:T(128)} %copy-done.1) | copy-start | bytes 580 | tf_op jit(solution)/shard_map/while
  433.1 0.6 copy-start.1
  500.5 9.5 %copy-start.2 = (s32[48]{0:T(128)S(1)}, s32[48]{0:T(128)}, u32[]{:S(2)}) copy-start(s32[48]{0:T(128)} %copy-done.1) | copy-start | bytes 580 | tf_op jit(solution)/shard_map/while
  510.0 0.6 copy-start.1
  577.8 9.5 %copy-start.2 = (s32[48]{0:T(128)S(1)}, s32[48]{0:T(128)}, u32[]{:S(2)}) copy-start(s32[48]{0:T(128)} %copy-done.1) | copy-start | bytes 580 | tf_op jit(solution)/shard_map/while
  596.2 8.8 %collective-permute-start.2 = (f32[7,128,128]{1,2,0:T(8,128)S(1)}, f32[7,128,128]{1,2,0:T(8,128)S(1)}, u32[]{:S(2)}, u32[]{:S(2)}) collective-permute-start(f32[7,128,128]{1,2,0:T(8,128)S(1)} %slice_bitcast_fusion.10), channel_id=1, source_target_pairs={{0,127},{1,0},{2,1},{3,2},{4,3},{5,4},{6,5},{7,6},{8,7},{9,8},{10,... | collective-permute-start | bytes 1376264 | tf_op jit(solution)/shard_map/ppermute | solution.py:9
  599.3 11.5 %collective-permute-start.3 = (f32[7,128,128]{2,1,0:T(8,128)S(1)}, f32[7,128,128]{2,1,0:T(8,128)S(1)}, u32[]{:S(2)}, u32[]{:S(2)}) collective-permute-start(f32[7,128,128]{2,1,0:T(8,128)S(1)} %dynamic-slice_bitcast_fusion), channel_id=1, source_target_pairs={{0,1},{1,2},{2,3},{3,4},{4,5},{5,6},{6,7},{7,8},{8,9},{9,10},{10,1... | collective-permute-start | bytes 1376264 | tf_op jit(solution)/shard_map/ppermute | solution.py:9
  617.4 71.2 %all-to-all-start = ((f32[12,7,16,8,128]{4,3,1,0,2:T(8,128)}), f32[12,7,16,8,128]{4,3,1,0,2:T(8,128)}, u32[]{:S(2)}, u32[]{:S(2)}) async-start(f32[12,7,16,8,128]{4,3,1,0,2:T(8,128)} %copy.80), calls=%async_computation | async-start | bytes 11010048 | tf_op jit(solution)/shard_map/all_to_all | solution.py:110
  625.5 88.4 %copy-start = (s32[8,2]{0,1:T(2,128)S(1)}, s32[8,2]{0,1:T(2,128)}, u32[]{:S(2)}) copy-start(s32[8,2]{0,1:T(2,128)} %param.13) | copy-start | bytes 196
  692.0 26.8 %collective-permute-start.4 = (f32[12,7,8,128]{3,2,1,0:T(8,128)S(1)}, f32[12,7,8,128]{3,2,1,0:T(8,128)}, u32[]{:S(2)}, u32[]{:S(2)}) collective-permute-start(f32[12,7,8,128]{3,2,1,0:T(8,128)S(1)} %get-tuple-element.275), channel_id=1, source_target_pairs={{0,16},{16,32},{32,48},{48,64},{64,80},{80,96},{96,112},{112,0},{1... | collective-permute-start | bytes 1032200 | tf_op jit(solution)/shard_map/ppermute | solution.py:9
  713.8 6.8 collective-permute-start.5
where the time goes:
time: 734 us; the launch traced here: 728 us
  other arithmetic  251 us (34%)
  waiting for transfers between devices  155 us (21%)
  local copies, waits for them, and re-layouts  112 us (15%)
  loops' own time  95.8 us (13%)
  matrix products  70.4 us (10%)
  starting transfers between devices  38.6 us (5%)
    dynamic_update_slice x48, other arithmetic, accumulate(): lax.dynamic_update_slice_in_dim(running, current + weighted, agg_block[li...  178 us
    ppermute x6, waiting for transfers between devices, passed_along(): lax.ppermute(shard, axis, [(i, (i + by) % devices) for i in range(devices)])  104 us
    another operation x1, loops' own time, local(): lax.fori_loop(0, slot_cap // block_rows, accumulate, jnp.zeros((agg_cap +...  95.8 us
    dot_general x6, matrix products, accumulate(): jnp.einsum('rkab,rkqbc->rkqac', a_block, gathered, preferred_element_type...  56.5 us
    gather x6, local copies, waits for them, and re-layouts, accumulate(): gathered = ghost_table[rows_block]  52.3 us
    all_to_all x1, waiting for transfers between devices, local(): lax.all_to_all(pieces, 'mem', split_axis=2, concat_axis=0, tiled=True)  50.8 us
    another operation x6, other arithmetic, accumulate(): jnp.stack([jnp.pad(triple[:, branch], ((0, 0), (2 - branch, branch), (0,...  34.7 us
    ppermute x6, starting transfers between devices, passed_along(): lax.ppermute(shard, axis, [(i, (i + by) % devices) for i in range(devices)])  30.6 us
  transfers between devices with their start and end apart: 7, of which 5 were waited for; matrix products, arithmetic and copies ran while one was open for 3% of the time, Pallas kernels for 0%

commit v1 on v0

v1 whole, which is shorter than its diff:
```python
import functools

import jax
import jax.numpy as jnp
from jax import lax
from jax.experimental import pallas as pl
from jax.experimental.pallas import tpu as pltpu
from jax.sharding import PartitionSpec as P

MESH = pl.DeviceIdType.MESH
F32 = jnp.float32
BF16 = jnp.bfloat16
KA = 7
KP = 3
BAND = 7
HALO = 4
WIDE = 5
CHUNK = 4
LONG = 8


def fused(sizes, a_hbm, p_hbm, offs, aggs, rows, flows, out_hbm,
          a_all, own, edge, ghost_out, ap, pt, band, near, send, recv, wide, outv, zsend, zrecv,
          start_tab, agg_tab, row_tab,
          a_sem, p_sem, halo_send, halo_recv, send_sem, recv_sem, self_sem, z_send, z_recv, out_sem):
    groups, members, cap, tile = sizes
    gmax = cap // 4
    pairs = gmax // 2
    coarse = members * gmax // 2
    fmax = coarse // 8
    out_cap = outv.shape[0]
    share = tile // members
    slots = gmax + 2
    spill = pairs * BAND
    total = spill + WIDE
    inner = cap - 2 * HALO
    grp = lax.axis_index("grp")
    mem = lax.axis_index("mem")
    up, down = lax.rem(grp + 1, groups), lax.rem(grp + groups - 1, groups)
    last = (mem == members - 1).astype(jnp.int32)
    first = (mem == 0).astype(jnp.int32)
    next_dev = (lax.rem(grp + last, groups), lax.rem(mem + 1, members))
    prev_dev = (lax.rem(grp + groups - first, groups), lax.rem(mem + members - 1, members))

    def p_copy(r):
        return pltpu.make_async_copy(p_hbm.at[r], own.at[pl.ds(WIDE * r + 2, KP)], p_sem)

    def a_copy(c):
        return pltpu.make_async_copy(
            a_hbm.at[pl.ds(c * CHUNK, CHUNK)], a_all.at[pl.ds(c * CHUNK, CHUNK)], a_sem.at[c])

    lax.fori_loop(0, cap, lambda r, _: (p_copy(r).start(), 0)[1], 0)
    lax.fori_loop(0, cap // CHUNK, lambda c, _: (a_copy(c).start(), 0)[1], 0)

    barrier = pltpu.get_barrier_semaphore()

    def greet(step, _):
        pl.semaphore_signal(barrier, inc=1, device_id=(grp, lax.rem(mem + step, members)), device_id_type=MESH)
        return 0

    lax.fori_loop(1, members, greet, 0)
    for device in ((up, mem), (down, mem), next_dev, prev_dev):
        pl.semaphore_signal(barrier, inc=1, device_id=device, device_id_type=MESH)

    n = rows[grp, mem]
    ga = aggs[grp, mem]

    def fill_agg(r, carry):
        agg, rest = carry
        agg_tab[r] = agg
        rest = rest + ga
        step = (rest >= n).astype(jnp.int32)
        return jnp.minimum(agg + step, gmax), rest - step * n

    lax.fori_loop(0, cap, fill_agg, (jnp.int32(0), jnp.int32(0)))

    def fill_start(a, carry):
        q, rest = carry
        start_tab[a] = jnp.minimum(q + (rest > 0).astype(jnp.int32), n)
        rest = rest + n
        for _ in range(LONG):
            step = (rest >= ga).astype(jnp.int32)
            q, rest = q + step, rest - step * ga
        return q, rest

    lax.fori_loop(0, gmax + 2, fill_start, (jnp.int32(0), jnp.int32(0)))

    def fill_row(c, carry):
        who, place = carry
        count = aggs[grp, who]
        slot = jnp.where(place < 2, gmax - 4 + place,
                         jnp.where(place >= count - 2, gmax + place - count, gmax - 2 + place - count))
        row_tab[c] = who * slots + jnp.clip(slot, 0, gmax - 1)
        done = (place + 1 >= count).astype(jnp.int32)
        return jnp.minimum(who + done, members - 1), (1 - done) * (place + 1)

    lax.fori_loop(0, coarse, fill_row, (jnp.int32(0), jnp.int32(0)))

    blank = jnp.zeros((tile, tile), BF16)

    def blank_row(table):
        def body(r, _):
            table[WIDE * r] = blank
            table[WIDE * r + 1] = blank
            return 0
        return body

    lax.fori_loop(0, cap + 1, blank_row(own), 0)
    lax.fori_loop(0, 6 * HALO + 1, blank_row(edge), 0)
    pt[cap] = jnp.zeros((KP * tile, tile), BF16)

    def blank_band(s, _):
        band[s] = jnp.zeros((BAND, tile, tile), F32)
        return 0

    lax.fori_loop(0, gmax + 2, blank_band, 0)

    whole = own.at[pl.ds(0, KP * cap)]
    pltpu.make_async_copy(whole, whole, p_sem).wait()
    for r in range(HALO):
        for q in range(KP):
            ghost_out[KP * r + q] = own[WIDE * jnp.maximum(n - HALO + r, 0) + 2 + q]
    pl.semaphore_wait(barrier, members - 1 + 4)

    def to_next(r):
        return pltpu.make_async_remote_copy(
            src_ref=ghost_out.at[pl.ds(KP * r, KP)], dst_ref=edge.at[pl.ds(WIDE * r + 2, KP)],
            send_sem=halo_send.at[r], recv_sem=halo_recv.at[r], device_id=next_dev, device_id_type=MESH)

    def to_prev(r):
        return pltpu.make_async_remote_copy(
            src_ref=own.at[pl.ds(WIDE * r + 2, KP)], dst_ref=edge.at[pl.ds(WIDE * (5 * HALO + r) + 2, KP)],
            send_sem=halo_send.at[HALO + r], recv_sem=halo_recv.at[HALO + r],
            device_id=prev_dev, device_id_type=MESH)

    for r in range(HALO):
        to_next(r).start()
        to_prev(r).start()

    for r in range(2 * HALO):
        for q in range(KP):
            edge[WIDE * (HALO + r) + 2 + q] = own[WIDE * r + 2 + q]
            edge[WIDE * (3 * HALO + r) + 2 + q] = own[WIDE * jnp.maximum(n - 2 * HALO + r, 0) + 2 + q]

    def ap_row(position, row, table, index_of):
        agg = agg_tab[row]
        begin, end = start_tab[agg], start_tab[agg + 1]
        bases = []
        for k in range(KA):
            target = row + offs[k, row]
            delta = (target >= end).astype(jnp.int32) - (target < begin).astype(jnp.int32)
            bases.append(WIDE * index_of(target) + 1 - delta)
        lhs = jnp.concatenate([a_all[row, k] for k in range(KA)], axis=1)
        for low, high in ((0, 2), (2, 4), (4, 5)):
            rhs = jnp.concatenate(
                [jnp.concatenate([table[b + e] for e in range(low, high)], axis=1) for b in bases], axis=0)
            out = jnp.dot(lhs, rhs, preferred_element_type=F32).astype(BF16)
            for e in range(low, high):
                ap[position, e] = out[:, (e - low) * tile:(e - low + 1) * tile]
        for q in range(KP):
            pt[position, pl.ds(q * tile, tile), :] = own[WIDE * row + 2 + q].T

    def inner_index(target):
        return jnp.clip(target, 0, cap - 1)

    def edge_index(target):
        from_end = 5 * HALO + target - n
        index = jnp.where(jnp.logical_or(target >= n, target >= 2 * HALO), from_end, HALO + target)
        return jnp.clip(index, 0, 6 * HALO - 1)

    def place_of(row):
        place = jnp.where(row < HALO, inner + row, jnp.where(row >= n - HALO, cap - n + row, row - HALO))
        return jnp.clip(place, 0, cap - 1)

    def products(begin, end, put):
        left, right = [], []
        for t in range(LONG):
            live = begin + t < end
            place = place_of(begin + t)
            left.append(jnp.where(live, place, cap))
            right.append(jnp.where(live, place, 0))
        lhs = jnp.concatenate([pt[i] for i in left], axis=1)
        for low, high in ((0, 2), (2, 4), (4, 5)):
            rhs = jnp.concatenate(
                [jnp.concatenate([ap[i, e] for e in range(low, high)], axis=1) for i in right], axis=0)
            out = jnp.dot(lhs, rhs, preferred_element_type=F32)
            for e in range(low, high):
                for q in range(KP):
                    put(q, e, out[q * tile:(q + 1) * tile, (e - low) * tile:(e - low + 1) * tile])

    def aggregate(back):
        agg = back + ga - gmax
        begin = start_tab[jnp.maximum(agg, 0)]
        end = jnp.where(agg >= 1, start_tab[jnp.maximum(agg, 0) + 1], 0)

        def put(q, e, value):
            band[back + q, e - q + 2] += value

        products(begin, end, put)

    def pack(upper, lower):
        both = jnp.concatenate(
            [upper.reshape(members, share, tile), lower.reshape(members, share, tile)], axis=1)
        return both.astype(BF16)

    def piece(step, begin, size, index):
        who = lax.rem(mem + step, members)
        return pltpu.make_async_remote_copy(
            src_ref=send.at[who, pl.ds(begin, size)], dst_ref=recv.at[mem, pl.ds(begin, size)],
            send_sem=send_sem.at[step - 1], recv_sem=recv_sem.at[index, step - 1],
            device_id=(grp, who), device_id_type=MESH)

    def kept(begin, size, index):
        return pltpu.make_async_copy(
            send.at[mem, pl.ds(begin, size)], recv.at[mem, pl.ds(begin, size)], self_sem.at[index])

    def send_out(begin, size, index):
        lax.fori_loop(1, members, lambda s, _: (piece(s, begin, size, index).start(), 0)[1], 0)
        kept(begin, size, index).start()

    def turn(w, _):
        def quarter(h, _):
            a_copy(1 + 2 * w + h).wait()
            for t in range(CHUNK):
                position = 2 * CHUNK * w + CHUNK * h + t
                ap_row(position, HALO + position, own, inner_index)
            return 0

        lax.fori_loop(0, 2, quarter, 0)
        aggregate(1 + 2 * w)
        aggregate(2 + 2 * w)

        @pl.when(w >= 1)
        def _():
            for o in range(BAND):
                send[:, (w - 1) * BAND + o] = pack(band[1 + 2 * w, o], band[2 + 2 * w, o])
            send_out((w - 1) * BAND, BAND, w - 1)
        return 0

    lax.fori_loop(0, inner // (2 * CHUNK), turn, 0)

    for c in (0, cap // CHUNK - 1):
        a_copy(c).wait()
    for r in range(HALO):
        to_next(r).wait_recv()
        to_prev(r).wait_recv()

    def edge_rows(h, _):
        for t in range(CHUNK):
            place = h * CHUNK + t
            row = jnp.where(place < HALO, place, jnp.maximum(n - 2 * HALO + place, 0))
            ap_row(inner + place, row, edge, edge_index)
        return 0

    lax.fori_loop(0, 2 * HALO // CHUNK, edge_rows, 0)
    aggregate(gmax - 1)

    def put_near(q, e, value):
        near[q, e] = value

    products(start_tab[0], start_tab[1], put_near)
    shift = jnp.clip(gmax - ga, 0, gmax - 1) + 1
    for o in range(BAND):
        upper, lower = band[shift, o], band[shift + 1, o]
        if 1 <= o <= WIDE:
            upper = upper + near[1, o - 1]
        if o < WIDE:
            lower = lower + near[2, o]
        send[:, (pairs - 2) * BAND + o] = pack(upper, lower)
    send_out((pairs - 2) * BAND, BAND, pairs - 2)
    for o in range(BAND):
        send[:, (pairs - 1) * BAND + o] = pack(band[gmax - 1, o], band[gmax, o])
    send_out((pairs - 1) * BAND, BAND, pairs - 1)
    for e in range(WIDE):
        send[:, spill + e] = pack(near[0, e], band[gmax + 1, e] + jnp.where(ga == 1, near[2, e], 0.0))
    send_out(spill, WIDE, pairs)

    def arrive(begin, size, index):
        lax.fori_loop(1, members, lambda s, _: (piece(s, begin, size, index).wait_recv(), 0)[1], 0)
        kept(begin, size, index).wait()

    def unpack(u, _):
        arrive(u * BAND, BAND, u)

        def body(who, _):
            for o in range(BAND):
                both = recv[who, u * BAND + o].astype(F32)
                wide[who * slots + 2 * u, o] = both[:share]
                wide[who * slots + 2 * u + 1, o] = both[share:]
            return 0

        return lax.fori_loop(0, members, body, 0)

    lax.fori_loop(0, pairs, unpack, 0)
    arrive(spill, WIDE, pairs)

    def unpack_spill(who, _):
        for e in range(WIDE):
            both = recv[who, spill + e].astype(F32)
            wide[who * slots + gmax, e + 2] = both[:share]
            wide[who * slots + gmax + 1, e] = both[share:]
        return 0

    lax.fori_loop(0, members, unpack_spill, 0)

    def add_spill(who, _):
        base, after = who * slots, (who + 1) * slots
        count = aggs[grp, who]
        for e in range(WIDE):
            wide[after + gmax - 4, e] += wide[base + gmax + 1, e]
            value = wide[after + gmax, e + 2]
            wide[base + gmax - 1, e + 2] += value
            wide[base + gmax - 4, e + 2] += jnp.where(count == 1, value, 0.0)
            wide[base + gmax - 3, e + 2] += jnp.where(count == 2, value, 0.0)
        return 0

    lax.fori_loop(0, members - 1, add_spill, 0)

    def z_pack(h, _):
        for way, base in ((0, coarse - fmax), (1, 0)):
            one = wide[row_tab[jnp.minimum(base + 2 * h, coarse - 1)]]
            two = wide[row_tab[jnp.minimum(base + 2 * h + 1, coarse - 1)]]
            for o in range(BAND):
                zsend[way, h * BAND + o] = jnp.concatenate([one[o], two[o]], axis=0).astype(BF16)
        return 0

    lax.fori_loop(0, (fmax + 1) // 2, z_pack, 0)
    ways = [
        pltpu.make_async_remote_copy(
            src_ref=zsend.at[way], dst_ref=zrecv.at[way], send_sem=z_send.at[way], recv_sem=z_recv.at[way],
            device_id=(group, mem), device_id_type=MESH)
        for way, group in ((0, up), (1, down))
    ]
    for way in ways:
        way.start()

    take_lower = flows[0, down]
    take_upper = flows[1, up]
    give_back = flows[1, grp]
    middle = coarse - flows[0, grp] - give_back
    foreign = members * slots
    wide[foreign + 2 * fmax + 2] = jnp.zeros((BAND, share, tile), F32)

    def gather(slot):
        row = jnp.where(slot < take_lower, slot - take_lower,
                        jnp.where(slot < take_lower + middle, give_back + slot - take_lower,
                                  coarse + slot - take_lower - middle))
        native = row_tab[jnp.clip(row, 0, coarse - 1)]
        where = jnp.where(row < 0, foreign + fmax + row,
                          jnp.where(row >= coarse, foreign + fmax + 1 + row - coarse, native))
        live = slot < take_lower + middle + take_upper
        index = jnp.where(live, where, foreign + 2 * fmax + 2)
        outv[slot] = wide[jnp.clip(index, 0, foreign + 2 * fmax + 2)]

    def gather_all(begin, end):
        def body(h, _):
            for t in range(4):
                gather(jnp.minimum(begin + 4 * h + t, end - 1))
            return 0
        lax.fori_loop(0, (end - begin + 3) // 4, body, 0)

    def out_copy(begin, end, index):
        return pltpu.make_async_copy(
            outv.at[pl.ds(begin, end - begin)], out_hbm.at[pl.ds(begin, end - begin)], out_sem.at[index])

    tail = 1 + coarse - 2 * fmax
    gather_all(fmax, tail)
    out_copy(fmax, tail, 0).start()
    for way in ways:
        way.wait()

    def z_unpack(h, _):
        for way, base in ((0, foreign), (1, foreign + fmax + 1)):
            for o in range(BAND):
                both = zrecv[way, h * BAND + o].astype(F32)
                wide[base + 2 * h, o] = both[:share]
                wide[base + 2 * h + 1, o] = both[share:]
        return 0

    lax.fori_loop(0, (fmax + 1) // 2, z_unpack, 0)
    for e in range(WIDE):
        wide[foreign + fmax - 1, e + 2] += wide[gmax, e + 2]
        wide[foreign + fmax + 1, e] += wide[foreign - 1, e]
    gather_all(0, fmax)
    gather_all(tail, out_cap)
    out_copy(0, fmax, 1).start()
    out_copy(tail, out_cap, 2).start()
    lax.fori_loop(1, members, lambda s, _: (piece(s, 0, total, 0).wait_send(), 0)[1], 0)
    for r in range(HALO):
        to_next(r).wait_send()
        to_prev(r).wait_send()
    for begin, end, index in ((fmax, tail, 0), (0, fmax, 1), (tail, out_cap, 2)):
        out_copy(begin, end, index).wait()


def local(a_tiles, p_tiles, a_offsets, agg_counts, row_counts, flows):
    cap, _, tile, _ = a_tiles.shape
    groups, members = lax.axis_size("grp"), lax.axis_size("mem")
    gmax = cap // 4
    pairs = gmax // 2
    coarse = members * gmax // 2
    fmax = coarse // 8
    share = tile // members
    pieces = pairs * BAND + WIDE
    out_cap = coarse + 2 * fmax - 2
    handed = (fmax + 1) // 2 * BAND
    smem = pl.BlockSpec(memory_space=pltpu.SMEM)
    hbm = pl.BlockSpec(memory_space=pl.ANY)
    return pl.pallas_call(
        functools.partial(fused, (groups, members, cap, tile)),
        out_shape=jax.ShapeDtypeStruct((out_cap, BAND, share, tile), F32),
        in_specs=[hbm, hbm, smem, smem, smem, smem],
        out_specs=hbm,
        scratch_shapes=[
            pltpu.VMEM((cap, KA, tile, tile), BF16),
            pltpu.VMEM((WIDE * cap + 2, tile, tile), BF16),
            pltpu.VMEM((WIDE * 6 * HALO + 2, tile, tile), BF16),
            pltpu.VMEM((HALO * KP, tile, tile), BF16),
            pltpu.VMEM((cap, WIDE, tile, tile), BF16),
            pltpu.VMEM((cap + 1, KP * tile, tile), BF16),
            pltpu.VMEM((gmax + 2, BAND, tile, tile), F32),
            pltpu.VMEM((KP, WIDE, tile, tile), F32),
            pltpu.VMEM((members, pieces, 2 * share, tile), BF16),
            pltpu.VMEM((members, pieces, 2 * share, tile), BF16),
            pltpu.VMEM((members * (gmax + 2) + 2 * fmax + 3, BAND, share, tile), F32),
            pltpu.VMEM((out_cap, BAND, share, tile), F32),
            pltpu.VMEM((2, handed, 2 * share, tile), BF16),
            pltpu.VMEM((2, handed, 2 * share, tile), BF16),
            pltpu.SMEM((gmax + 2,), jnp.int32),
            pltpu.SMEM((cap,), jnp.int32),
            pltpu.SMEM((coarse,), jnp.int32),
            pltpu.SemaphoreType.DMA((cap // CHUNK,)),
            pltpu.SemaphoreType.DMA,
            pltpu.SemaphoreType.DMA((2 * HALO,)),
            pltpu.SemaphoreType.DMA((2 * HALO,)),
            pltpu.SemaphoreType.DMA((members - 1,)),
            pltpu.SemaphoreType.DMA((pairs + 1, members - 1)),
            pltpu.SemaphoreType.DMA((pairs + 1,)),
            pltpu.SemaphoreType.DMA((2,)),
            pltpu.SemaphoreType.DMA((2,)),
            pltpu.SemaphoreType.DMA((3,)),
        ],
        compiler_params=pltpu.CompilerParams(
            collective_id=0, has_side_effects=True, vmem_limit_bytes=62 * 1024 * 1024),
        cost_estimate=pl.CostEstimate(flops=7_500_000_000, bytes_accessed=20_000_000, transcendentals=0),
    )(a_tiles, p_tiles, a_offsets.T, agg_counts, row_counts, flows.T)


def solution(mesh):
    placed = (
        P(("grp", "mem"), None, None, None),
        P(("grp", "mem"), None, None, None),
        P(("grp", "mem"), None),
        P(),
        P(),
        P(),
    )
    return jax.shard_map(
        local, mesh=mesh, in_specs=placed, out_specs=P("grp", None, "mem", None), check_vma=False
    )
```

time: 734 us -> 67.1 us (0.09)
  other arithmetic: 251 us -> 0 us
  waiting for transfers between devices: 155 us -> 0 us
  local copies, waits for them, and re-layouts: 112 us -> 3.92 us
  loops' own time: 95.8 us -> 0 us
  matrix products: 70.4 us -> 0 us
  Pallas kernels: 0 us -> 62.5 us
  starting transfers between devices: 38.6 us -> 0 us
    dynamic_update_slice x48 -> x0, other arithmetic: 178 us -> none  [accumulate(): lax.dynamic_update_slice_in_dim(running, current + weighted, agg_block[li...]
    ppermute x6 -> x0, waiting for transfers between devices: 104 us -> none  [passed_along(): lax.ppermute(shard, axis, [(i, (i + by) % devices) for i in range(devices)])]
    another operation x1 -> x0, loops' own time: 95.8 us -> none  [local(): lax.fori_loop(0, slot_cap // block_rows, accumulate, jnp.zeros((agg_cap +...]
    dot_general x12 -> x0, matrix products: 70.4 us -> none  [the longest x6 56.5 us: accumulate(): jnp.einsum('rkab,rkqbc->rkqac', a_block, gathered, preferred_element_type...]
    pallas_call x0 -> x1, Pallas kernels: none -> 62.5 us  [local(): pl.pallas_call(functools.partial(fused, (groups, members, cap, tile)), ou...]
    gather x9 -> x0, local copies, waits for them, and re-layouts: 59 us -> none  [the longest x6 52.3 us: accumulate(): gathered = ghost_table[rows_block]]
    all_to_all x1 -> x0, waiting for transfers between devices: 50.8 us -> none  [local(): lax.all_to_all(pieces, 'mem', split_axis=2, concat_axis=0, tiled=True)]
    another operation x8 -> x0, other arithmetic: 34.9 us -> none  [the longest x6 34.7 us: accumulate(): jnp.stack([jnp.pad(triple[:, branch], ((0, 0), (2 - branch, branch), (0,...]
  transfers between devices with their start and end apart: 7 -> 0, of which waited for: 5 -> 0; matrix products, arithmetic and copies ran while one was open for 3% -> 0% of each run, Pallas kernels for 0% -> 0%
where the time goes in v1:
time: 67.1 us; the launch traced here: 66.5 us
  Pallas kernels  62.5 us (93%)
  local copies, waits for them, and re-layouts  3.92 us (6%)
    pallas_call x1, Pallas kernels, local(): pl.pallas_call(functools.partial(fused, (groups, members, cap, tile)), ou...  62.5 us
    unnamed x1, local copies, waits for them, and re-layouts  3.92 us

profile of v1, /device:TPU:1, one launch (start us, length us, event | category | flops | bytes accessed | tf_op | source)
XLA Modules:
  0.0 66.5 jit_solution(12163039246197945253)
XLA Ops:
  0.0 62.5 %shard_map.64 = f32[118,7,8,128]{3,2,1,0:T(8,128)} custom-call(bf16[48,7,128,128]{3,2,1,0:T(8,128)(2,1)} %a_hbm.1, bf16[48,3,128,128]{3,2,1,0:T(8,128)(2,1)} %p_hbm.1, s32[7,48]{1,0:T(8,128)} %bitcast.2, s32[8,16]{1,0:T(8,128)} %aggs.1, s32[8,16]{1,0:T(8,128)} %rows.1, s32[2,8]{1,0:T(2,128)} %bitcast.3), custom_call_target="tpu_custom_call" | custom-call | flops 7500000256 | bytes 20000000 | tf_op jit(solution)/shard_map/pallas_call | solution.py:409
  62.5 3.9 %copy.8 = f32[118,7,8,128]{3,2,1,0:T(8,128)} copy(f32[118,7,8,128]{3,2,1,0:T(8,128)} %shard_map.64) | data formatting | bytes 6766592

commit v2 on v1

v2 whole, which is shorter than its diff:
```python
import functools

import jax
import jax.numpy as jnp
from jax import lax
from jax.experimental import pallas as pl
from jax.experimental.pallas import tpu as pltpu
from jax.sharding import PartitionSpec as P

MESH = pl.DeviceIdType.MESH
F32 = jnp.float32
BF16 = jnp.bfloat16
KA = 7
KP = 3
BAND = 7
HALO = 4
WIDE = 5
STRIDE = 6
LEAD = STRIDE - KP
CHUNK = 4
LONG = 8
EARLY = 8


def fused(sizes, a_hbm, p_hbm, offs, aggs, rows, flows, outv,
          a_early, a_all, own, edge, ghost_out, ap, pt, band, near, send, recv, foreign, zsend, zrecv,
          start_tab, agg_tab, slot_tab, who_tab,
          a_sem, p_sem, halo_send, halo_recv, send_sem, recv_sem, self_sem, z_send, z_recv):
    groups, members, cap, tile = sizes
    gmax = cap // 4
    pairs = gmax // 2
    coarse = members * gmax // 2
    fmax = coarse // 8
    out_cap = outv.shape[0]
    share = tile // members
    side = 2 if members == 4 else 4
    spill = pairs * BAND
    total = spill + WIDE
    inner = cap - 2 * HALO
    grp = lax.axis_index("grp")
    mem = lax.axis_index("mem")
    up, down = lax.rem(grp + 1, groups), lax.rem(grp + groups - 1, groups)
    last = (mem == members - 1).astype(jnp.int32)
    first = (mem == 0).astype(jnp.int32)
    next_dev = (lax.rem(grp + last, groups), lax.rem(mem + 1, members))
    prev_dev = (lax.rem(grp + groups - first, groups), lax.rem(mem + members - 1, members))

    def p_copy(r):
        return pltpu.make_async_copy(p_hbm.at[pl.ds(KP * r, KP)], own.at[pl.ds(STRIDE * r + LEAD, KP)], p_sem)

    early = pltpu.make_async_copy(
        a_hbm.at[pl.ds(KA * HALO, KA * EARLY)], a_early.at[pl.ds(0, KA * EARLY)], a_sem.at[0])
    whole_a = pltpu.make_async_copy(a_hbm, a_all.at[pl.ds(0, KA * cap)], a_sem.at[1])
    lax.fori_loop(0, cap, lambda r, _: (p_copy(r).start(), 0)[1], 0)
    early.start()
    whole_a.start()

    barrier = pltpu.get_barrier_semaphore()

    def greet(step, _):
        pl.semaphore_signal(barrier, inc=1, device_id=(grp, lax.rem(mem + step, members)), device_id_type=MESH)
        return 0

    lax.fori_loop(1, members, greet, 0)
    for device in ((up, mem), (down, mem), next_dev, prev_dev):
        pl.semaphore_signal(barrier, inc=1, device_id=device, device_id_type=MESH)

    n = rows[grp, mem]
    ga = aggs[grp, mem]

    def fill_agg(r, carry):
        agg, rest = carry
        agg_tab[r] = agg
        rest = rest + ga
        step = (rest >= n).astype(jnp.int32)
        return jnp.minimum(agg + step, gmax), rest - step * n

    lax.fori_loop(0, cap + 1, fill_agg, (jnp.int32(0), jnp.int32(0)))

    def fill_start(a, carry):
        q, rest = carry
        start_tab[a] = jnp.where(a > ga, 2 * cap, q + (rest > 0).astype(jnp.int32))
        rest = rest + n
        for _ in range(LONG):
            step = (rest >= ga).astype(jnp.int32)
            q, rest = q + step, rest - step * ga
        return q, rest

    lax.fori_loop(0, gmax + 3, fill_start, (jnp.int32(0), jnp.int32(0)))

    def fill_row(c, carry):
        who, place = carry
        count = aggs[grp, who]
        slot = jnp.where(place < 2, gmax - 4 + place,
                         jnp.where(place >= count - 2, gmax + place - count, gmax - 2 + place - count))
        slot_tab[c] = jnp.clip(slot, 0, gmax - 1)
        who_tab[c] = who
        done = (place + 1 >= count).astype(jnp.int32)
        return jnp.minimum(who + done, members - 1), (1 - done) * (place + 1)

    lax.fori_loop(0, coarse, fill_row, (jnp.int32(0), jnp.int32(0)))

    blank = jnp.zeros((tile, tile), BF16)

    def blank_row(table):
        def body(r, _):
            for e in range(LEAD):
                table[STRIDE * r + e] = blank
            return 0
        return body

    lax.fori_loop(0, cap + 1, blank_row(own), 0)
    lax.fori_loop(0, 6 * HALO + 1, blank_row(edge), 0)
    pt[cap] = jnp.zeros((KP * tile, tile), BF16)
    a_early[KA * EARLY] = blank
    a_all[KA * cap] = blank

    def blank_band(s, _):
        band[s] = jnp.zeros((BAND, members, share, tile), F32)
        return 0

    lax.fori_loop(0, gmax + 2, blank_band, 0)

    whole = own.at[pl.ds(0, KP * cap)]
    pltpu.make_async_copy(whole, whole, p_sem).wait()

    def to_next(r):
        return pltpu.make_async_remote_copy(
            src_ref=ghost_out.at[pl.ds(KP * r, KP)], dst_ref=edge.at[pl.ds(STRIDE * r + LEAD, KP)],
            send_sem=halo_send.at[r], recv_sem=halo_recv.at[r], device_id=next_dev, device_id_type=MESH)

    def to_prev(r):
        return pltpu.make_async_remote_copy(
            src_ref=own.at[pl.ds(STRIDE * r + LEAD, KP)],
            dst_ref=edge.at[pl.ds(STRIDE * (5 * HALO + r) + LEAD, KP)],
            send_sem=halo_send.at[HALO + r], recv_sem=halo_recv.at[HALO + r],
            device_id=prev_dev, device_id_type=MESH)

    def halo_out():
        for r in range(HALO):
            for q in range(KP):
                ghost_out[KP * r + q] = own[STRIDE * jnp.maximum(n - HALO + r, 0) + LEAD + q]
        pl.semaphore_wait(barrier, members - 1 + 4)
        for r in range(HALO):
            to_next(r).start()
            to_prev(r).start()
        for r in range(2 * HALO):
            for q in range(KP):
                edge[STRIDE * (HALO + r) + LEAD + q] = own[STRIDE * r + LEAD + q]
                edge[STRIDE * (3 * HALO + r) + LEAD + q] = own[STRIDE * jnp.maximum(n - 2 * HALO + r, 0) + LEAD + q]

    def ap_pair(position, row, a_ref, a_first, blank_tile, table, index_of):
        agg = agg_tab[row]
        begin, end, beyond = start_tab[agg], start_tab[agg + 1], start_tab[agg + 2]
        window = 2 * HALO + 2
        bases = []
        for w in range(window):
            target = row - HALO + w
            ahead = ((target >= end).astype(jnp.int32) + (target >= beyond).astype(jnp.int32)
                     - (target < begin).astype(jnp.int32))
            bases.append(STRIDE * index_of(target) + LEAD - 1 - ahead)

        def tile_at(line, offset):
            base = KA * (line - a_first)
            if offset == 0:
                return a_ref[base]
            index = jnp.int32(blank_tile)
            if abs(offset) <= HALO:
                for k in range(1, KA):
                    index = jnp.where(offs[k, line] == offset, base + k, index)
            return a_ref[index]

        lhs = jnp.concatenate(
            [jnp.concatenate([tile_at(row, w - HALO), tile_at(row + 1, w - HALO - 1)], axis=0)
             for w in range(window)], axis=1)
        same = agg_tab[row + 1] == agg
        lower = []
        for low, from_w in ((0, 0), (2, 0), (4, HALO)):
            rhs = jnp.concatenate(
                [jnp.concatenate([table[b + low], table[b + low + 1]], axis=1) for b in bases[from_w:]], axis=0)
            out = jnp.dot(lhs[:, from_w * tile:], rhs, preferred_element_type=F32)
            for e in (0, 1):
                if low + e < WIDE:
                    ap[position, low + e] = out[:tile, e * tile:(e + 1) * tile].astype(BF16)
                lower.append(out[tile:, e * tile:(e + 1) * tile])
        for e in range(WIDE):
            ap[position + 1, e] = jnp.where(same, lower[e], lower[e + 1]).astype(BF16)
        for t in (0, 1):
            for q in range(KP):
                pt[position + t, pl.ds(q * tile, tile), :] = own[STRIDE * (row + t) + LEAD + q].T

    def inner_index(target):
        return jnp.clip(target, 0, cap - 1)

    def edge_index(target):
        from_end = 5 * HALO + target - n
        index = jnp.where(jnp.logical_or(target >= n, target >= 2 * HALO), from_end, HALO + target)
        return jnp.clip(index, 0, 6 * HALO - 1)

    def place_of(row):
        place = jnp.where(row < HALO, inner + row, jnp.where(row >= n - HALO, cap - n + row, row - HALO))
        return jnp.clip(place, 0, cap - 1)

    def products(begin, end, put):
        left, right = [], []
        for t in range(LONG):
            live = begin + t < end
            place = place_of(begin + t)
            left.append(jnp.where(live, place, cap))
            right.append(jnp.where(live, place, 0))
        lhs = jnp.concatenate([pt[i] for i in left], axis=1)
        for low, high in ((0, 2), (2, 4), (4, 5)):
            rhs = jnp.concatenate(
                [jnp.concatenate([ap[i, e] for e in range(low, high)], axis=1) for i in right], axis=0)
            out = jnp.dot(lhs, rhs, preferred_element_type=F32)
            for e in range(low, high):
                for q in range(KP):
                    part = out[q * tile:(q + 1) * tile, (e - low) * tile:(e - low + 1) * tile]
                    put(q, e, part.reshape(members, share, tile))

    def aggregate(back):
        agg = back + ga - gmax
        begin = start_tab[jnp.maximum(agg, 0)]
        end = jnp.where(agg >= 1, start_tab[jnp.maximum(agg, 0) + 1], 0)

        def put(q, e, value):
            band[back + q, e - q + 2] += value

        products(begin, end, put)

    def pack(upper, lower):
        return jnp.concatenate([upper, lower], axis=1).astype(BF16)

    def piece(step, begin, size, index):
        away = lax.rem(step * 7, members)
        who = (lax.rem(mem // side + away // side, side) * side
               + lax.rem(lax.rem(mem, side) + lax.rem(away, side), side))
        return pltpu.make_async_remote_copy(
            src_ref=send.at[who, pl.ds(begin, size)], dst_ref=recv.at[mem, pl.ds(begin, size)],
            send_sem=send_sem.at[step - 1], recv_sem=recv_sem.at[index, step - 1],
            device_id=(grp, who), device_id_type=MESH)

    def kept(begin, size, index):
        return pltpu.make_async_copy(
            send.at[mem, pl.ds(begin, size)], recv.at[mem, pl.ds(begin, size)], self_sem.at[index])

    def send_out(begin, size, index):
        lax.fori_loop(1, members, lambda s, _: (piece(s, begin, size, index).start(), 0)[1], 0)
        kept(begin, size, index).start()

    def quarter(position, a_ref, a_first, blank_tile):
        for t in range(0, CHUNK, 2):
            ap_pair(position + t, HALO + position + t, a_ref, a_first, blank_tile, own, inner_index)

    early.wait()
    lax.fori_loop(0, EARLY // CHUNK, lambda h, _: (quarter(CHUNK * h, a_early, HALO, KA * EARLY), 0)[1], 0)
    halo_out()
    aggregate(1)
    aggregate(2)
    whole_a.wait()

    def turn(w, _):
        lax.fori_loop(0, 2, lambda h, _: (quarter(2 * CHUNK * w + CHUNK * h, a_all, 0, KA * cap), 0)[1], 0)
        aggregate(1 + 2 * w)
        aggregate(2 + 2 * w)
        for o in range(BAND):
            send[:, (w - 1) * BAND + o] = pack(band[1 + 2 * w, o], band[2 + 2 * w, o])
        send_out((w - 1) * BAND, BAND, w - 1)
        return 0

    lax.fori_loop(1, inner // (2 * CHUNK), turn, 0)

    for r in range(HALO):
        to_next(r).wait_recv()
        to_prev(r).wait_recv()

    def edge_rows(h, _):
        for t in range(0, CHUNK, 2):
            place = h * CHUNK + t
            row = jnp.where(place < HALO, place, jnp.maximum(n - 2 * HALO + place, 0))
            ap_pair(inner + place, row, a_all, 0, KA * cap, edge, edge_index)
        return 0

    lax.fori_loop(0, 2 * HALO // CHUNK, edge_rows, 0)
    aggregate(gmax - 1)

    def put_near(q, e, value):
        near[q, e] = value

    products(start_tab[0], start_tab[1], put_near)
    shift = jnp.clip(gmax - ga, 0, gmax - 1) + 1
    for o in range(BAND):
        upper, lower = band[shift, o], band[shift + 1, o]
        if 1 <= o <= WIDE:
            upper = upper + near[1, o - 1]
        if o < WIDE:
            lower = lower + near[2, o]
        send[:, (pairs - 2) * BAND + o] = pack(upper, lower)
    send_out((pairs - 2) * BAND, BAND, pairs - 2)
    for o in range(BAND):
        send[:, (pairs - 1) * BAND + o] = pack(band[gmax - 1, o], band[gmax, o])
    send_out((pairs - 1) * BAND, BAND, pairs - 1)
    for e in range(WIDE):
        send[:, spill + e] = pack(near[0, e], band[gmax + 1, e] + jnp.where(ga == 1, near[2, e], 0.0))
    send_out(spill, WIDE, pairs)

    def arrive(begin, size, index):
        lax.fori_loop(1, members, lambda s, _: (piece(s, begin, size, index).wait_recv(), 0)[1], 0)
        kept(begin, size, index).wait()

    def unpack(u, _):
        arrive(u * BAND, BAND, u)

        def body(who, _):
            for o in range(BAND):
                both = recv[who, u * BAND + o].astype(F32)
                band[2 * u, o, who] = both[:share]
                band[2 * u + 1, o, who] = both[share:]
            return 0

        return lax.fori_loop(0, members, body, 0)

    lax.fori_loop(0, pairs, unpack, 0)
    arrive(spill, WIDE, pairs)

    def unpack_spill(who, _):
        for e in range(WIDE):
            both = recv[who, spill + e].astype(F32)
            band[gmax, e + 2, who] = both[:share]
            band[gmax + 1, e, who] = both[share:]
        return 0

    lax.fori_loop(0, members, unpack_spill, 0)

    def add_spill(who, _):
        here, after = who, who + 1
        count = aggs[grp, who]
        for e in range(WIDE):
            band[gmax - 4, e, after] += band[gmax + 1, e, here]
            value = band[gmax, e + 2, after]
            band[gmax - 1, e + 2, here] += value
            band[gmax - 4, e + 2, here] += jnp.where(count == 1, value, 0.0)
            band[gmax - 3, e + 2, here] += jnp.where(count == 2, value, 0.0)
        return 0

    lax.fori_loop(0, members - 1, add_spill, 0)

    def coarse_row(row):
        row = jnp.clip(row, 0, coarse - 1)
        slot, who = slot_tab[row], who_tab[row]
        return [band[slot, o, who] for o in range(BAND)]

    def z_pack(h, _):
        for way, base in ((0, coarse - fmax), (1, 0)):
            one, two = coarse_row(base + 2 * h), coarse_row(base + 2 * h + 1)
            for o in range(BAND):
                zsend[way, h * BAND + o] = jnp.concatenate([one[o], two[o]], axis=0).astype(BF16)
        return 0

    lax.fori_loop(0, (fmax + 1) // 2, z_pack, 0)
    ways = [
        pltpu.make_async_remote_copy(
            src_ref=zsend.at[way], dst_ref=zrecv.at[way], send_sem=z_send.at[way], recv_sem=z_recv.at[way],
            device_id=(group, mem), device_id_type=MESH)
        for way, group in ((0, up), (1, down))
    ]
    for way in ways:
        way.start()

    take_lower = flows[0, down]
    take_upper = flows[1, up]
    give_back = flows[1, grp]
    middle = coarse - flows[0, grp] - give_back
    foreign[2 * fmax + 2] = jnp.zeros((BAND, share, tile), F32)

    def place(slot):
        return jnp.where(slot < take_lower, slot - take_lower,
                         jnp.where(slot < take_lower + middle, give_back + slot - take_lower,
                                   coarse + slot - take_lower - middle))

    def in_middle(slot):
        for o, value in enumerate(coarse_row(place(slot))):
            outv[slot, o] = value

    def at_end(slot):
        row = place(slot)
        live = slot < take_lower + middle + take_upper
        native = jnp.logical_and(live, jnp.logical_and(row >= 0, row < coarse))
        index = jnp.where(live, jnp.where(row < 0, fmax + row, fmax + 1 + row - coarse), 2 * fmax + 2)
        other = foreign[jnp.clip(index, 0, 2 * fmax + 2)]
        for o, value in enumerate(coarse_row(row)):
            outv[slot, o] = jnp.where(native, value, other[o])

    def gather_all(fill, begin, end):
        def body(h, _):
            for t in range(4):
                fill(jnp.minimum(begin + 4 * h + t, end - 1))
            return 0
        lax.fori_loop(0, (end - begin + 3) // 4, body, 0)

    tail = 1 + coarse - 2 * fmax
    gather_all(in_middle, fmax, tail)
    for way in ways:
        way.wait()

    def z_unpack(h, _):
        for way, base in ((0, 0), (1, fmax + 1)):
            for o in range(BAND):
                both = zrecv[way, h * BAND + o].astype(F32)
                foreign[base + 2 * h, o] = both[:share]
                foreign[base + 2 * h + 1, o] = both[share:]
        return 0

    lax.fori_loop(0, (fmax + 1) // 2, z_unpack, 0)
    for e in range(WIDE):
        foreign[fmax - 1, e + 2] += band[gmax, e + 2, 0]
        foreign[fmax + 1, e] += band[gmax + 1, e, members - 1]
    gather_all(at_end, 0, fmax)
    gather_all(at_end, tail, out_cap)
    lax.fori_loop(1, members, lambda s, _: (piece(s, 0, total, 0).wait_send(), 0)[1], 0)
    for r in range(HALO):
        to_next(r).wait_send()
        to_prev(r).wait_send()


def write_out(held, out_hbm, sem):
    copy = pltpu.make_async_copy(held, out_hbm, sem)
    copy.start()
    copy.wait()


def local(a_tiles, p_tiles, a_offsets, agg_counts, row_counts, flows):
    cap, _, tile, _ = a_tiles.shape
    groups, members = lax.axis_size("grp"), lax.axis_size("mem")
    gmax = cap // 4
    pairs = gmax // 2
    coarse = members * gmax // 2
    fmax = coarse // 8
    share = tile // members
    pieces = pairs * BAND + WIDE
    out_cap = coarse + 2 * fmax - 2
    handed = (fmax + 1) // 2 * BAND
    smem = pl.BlockSpec(memory_space=pltpu.SMEM)
    hbm = pl.BlockSpec(memory_space=pl.ANY)
    vmem = pl.BlockSpec(memory_space=pltpu.VMEM)
    held = pl.pallas_call(
        functools.partial(fused, (groups, members, cap, tile)),
        out_shape=pltpu.VMEM((out_cap, BAND, share, tile), F32),
        in_specs=[hbm, hbm, smem, smem, smem, smem],
        out_specs=vmem,
        scratch_shapes=[
            pltpu.VMEM((KA * EARLY + 1, tile, tile), BF16),
            pltpu.VMEM((KA * cap + 1, tile, tile), BF16),
            pltpu.VMEM((STRIDE * cap + LEAD, tile, tile), BF16),
            pltpu.VMEM((STRIDE * 6 * HALO + LEAD, tile, tile), BF16),
            pltpu.VMEM((HALO * KP, tile, tile), BF16),
            pltpu.VMEM((cap, WIDE, tile, tile), BF16),
            pltpu.VMEM((cap + 1, KP * tile, tile), BF16),
            pltpu.VMEM((gmax + 2, BAND, members, share, tile), F32),
            pltpu.VMEM((KP, WIDE, members, share, tile), F32),
            pltpu.VMEM((members, pieces, 2 * share, tile), BF16),
            pltpu.VMEM((members, pieces, 2 * share, tile), BF16),
            pltpu.VMEM((2 * fmax + 3, BAND, share, tile), F32),
            pltpu.VMEM((2, handed, 2 * share, tile), BF16),
            pltpu.VMEM((2, handed, 2 * share, tile), BF16),
            pltpu.SMEM((gmax + 3,), jnp.int32),
            pltpu.SMEM((cap + 1,), jnp.int32),
            pltpu.SMEM((coarse,), jnp.int32),
            pltpu.SMEM((coarse,), jnp.int32),
            pltpu.SemaphoreType.DMA((2,)),
            pltpu.SemaphoreType.DMA,
            pltpu.SemaphoreType.DMA((2 * HALO,)),
            pltpu.SemaphoreType.DMA((2 * HALO,)),
            pltpu.SemaphoreType.DMA((members - 1,)),
            pltpu.SemaphoreType.DMA((pairs + 1, members - 1)),
            pltpu.SemaphoreType.DMA((pairs + 1,)),
            pltpu.SemaphoreType.DMA((2,)),
            pltpu.SemaphoreType.DMA((2,)),
        ],
        compiler_params=pltpu.CompilerParams(
            collective_id=0, has_side_effects=True, vmem_limit_bytes=58 * 1024 * 1024),
        cost_estimate=pl.CostEstimate(flops=7_500_000_000, bytes_accessed=20_000_000, transcendentals=0),
    )(a_tiles.reshape(cap * KA, tile, tile), p_tiles.reshape(cap * KP, tile, tile), a_offsets.T,
      agg_counts, row_counts, flows.T)
    return pl.pallas_call(
        write_out,
        out_shape=jax.ShapeDtypeStruct((out_cap, BAND, share, tile), F32),
        in_specs=[vmem],
        out_specs=hbm,
        scratch_shapes=[pltpu.SemaphoreType.DMA],
        cost_estimate=pl.CostEstimate(flops=0, bytes_accessed=6_800_000, transcendentals=0),
    )(held)


def solution(mesh):
    placed = (
        P(("grp", "mem"), None, None, None),
        P(("grp", "mem"), None, None, None),
        P(("grp", "mem"), None),
        P(),
        P(),
        P(),
    )
    return jax.shard_map(
        local, mesh=mesh, in_specs=placed, out_specs=P("grp", None, "mem", None), check_vma=False
    )
```

time: 67.1 us -> 69.6 us (1.037)
  Pallas kernels: 62.5 us -> 67.5 us
  local copies, waits for them, and re-layouts: 3.92 us -> 1.69 us
    pallas_call x0 -> x1, Pallas kernels: none -> 3.7 us  [local(): pl.pallas_call(write_out, out_shape=jax.ShapeDtypeStruct((out_cap, BAND,...]
    unnamed x1 -> x2, local copies, waits for them, and re-layouts: 3.92 us -> 1.69 us
    pallas_call x1, Pallas kernels: 62.5 us -> 63.8 us  [local(): pl.pallas_call(functools.partial(fused, (groups, members, cap, tile)), ou...]
where the time goes in v2:
time: 69.6 us; the launch traced here: 69.2 us
  Pallas kernels  67.5 us (97%)
  local copies, waits for them, and re-layouts  1.69 us (2%)
    pallas_call x1, Pallas kernels, local(): pl.pallas_call(functools.partial(fused, (groups, members, cap, tile)), ou...  63.8 us
    pallas_call x1, Pallas kernels, local(): pl.pallas_call(write_out, out_shape=jax.ShapeDtypeStruct((out_cap, BAND,...  3.7 us
    unnamed x2, local copies, waits for them, and re-layouts  1.69 us

profile of v2, /device:TPU:1, one launch (start us, length us, event | category | flops | bytes accessed | tf_op | source)
XLA Modules:
  0.0 69.2 jit_solution(11423873703759850717)
XLA Ops:
  0.0 63.8 %shard_map.64.held = f32[118,7,8,128]{3,2,1,0:T(8,128)S(1)} custom-call(bf16[336,128,128]{2,1,0:T(8,128)(2,1)} %bitcast.4, bf16[144,128,128]{2,1,0:T(8,128)(2,1)} %bitcast.5, s32[7,48]{1,0:T(8,128)} %bitcast.6, s32[8,16]{1,0:T(8,128)} %aggs.1, s32[8,16]{1,0:T(8,128)} %rows.1, s32[2,8]{1,0:T(2,128)} %bitcast.7), custom_call_target="tpu_custom_call" | custom-call | flops 7500000256 | bytes 20000000 | tf_op jit(solution)/shard_map/pallas_call | solution.py:446
  63.8 0.0 copy-start
  63.8 1.7 %copy-done = f32[118,7,8,128]{3,2,1,0:T(8,128)} copy-done((f32[118,7,8,128]{3,2,1,0:T(8,128)}, f32[118,7,8,128]{3,2,1,0:T(8,128)S(1)}, u32[]{:S(2)}) %copy-start) | copy-done | bytes 3383320
  65.5 3.7 %shard_map.65 = f32[118,7,8,128]{3,2,1,0:T(8,128)} custom-call(f32[118,7,8,128]{3,2,1,0:T(8,128)} %copy-done), custom_call_target="tpu_custom_call" | custom-call | bytes 6800000 | tf_op jit(solution)/shard_map/pallas_call | solution.py:485
Async XLA Ops:
  63.8 1.7 %copy-start = (f32[118,7,8,128]{3,2,1,0:T(8,128)}, f32[118,7,8,128]{3,2,1,0:T(8,128)S(1)}, u32[]{:S(2)}) copy-start(f32[118,7,8,128]{3,2,1,0:T(8,128)S(1)} %shard_map.64.held) | copy-start | bytes 10149892

commit v3 on v2

--- a/solution.py
+++ b/solution.py
@@ -23,7 +23,7 @@
 
 
 def fused(sizes, a_hbm, p_hbm, offs, aggs, rows, flows, outv,
-          a_early, a_all, own, edge, ghost_out, ap, pt, band, near, send, recv, foreign, zsend, zrecv,
+          a_early, a_mid, a_all, own, edge, ghost_out, ap, pt, band, near, send, recv, foreign, zsend, zrecv,
           start_tab, agg_tab, slot_tab, who_tab,
           a_sem, p_sem, halo_send, halo_recv, send_sem, recv_sem, self_sem, z_send, z_recv):
     groups, members, cap, tile = sizes
@@ -48,12 +48,22 @@
     def p_copy(r):
         return pltpu.make_async_copy(p_hbm.at[pl.ds(KP * r, KP)], own.at[pl.ds(STRIDE * r + LEAD, KP)], p_sem)
 
-    early = pltpu.make_async_copy(
-        a_hbm.at[pl.ds(KA * HALO, KA * EARLY)], a_early.at[pl.ds(0, KA * EARLY)], a_sem.at[0])
+    def a_copy(r):
+        return pltpu.make_async_copy(a_hbm.at[pl.ds(KA * r, KA)], a_all.at[pl.ds(KA * r, KA)], a_sem.at[1])
+
+    def early_copy(r, count):
+        return pltpu.make_async_copy(
+            a_hbm.at[pl.ds(KA * (HALO + r), KA * count)], a_early.at[pl.ds(KA * r, KA * count)], a_sem.at[0])
+
+    def mid_copy(r, count):
+        return pltpu.make_async_copy(
+            a_hbm.at[pl.ds(KA * (HALO + EARLY + r), KA * count)], a_mid.at[pl.ds(KA * r, KA * count)], a_sem.at[2])
+
     whole_a = pltpu.make_async_copy(a_hbm, a_all.at[pl.ds(0, KA * cap)], a_sem.at[1])
     lax.fori_loop(0, cap, lambda r, _: (p_copy(r).start(), 0)[1], 0)
-    early.start()
-    whole_a.start()
+    lax.fori_loop(0, EARLY, lambda r, _: (early_copy(r, 1).start(), 0)[1], 0)
+    lax.fori_loop(0, EARLY, lambda r, _: (mid_copy(r, 1).start(), 0)[1], 0)
+    lax.fori_loop(0, cap, lambda r, _: (a_copy(r).start(), 0)[1], 0)
 
     barrier = pltpu.get_barrier_semaphore()
 
@@ -88,17 +98,22 @@
 
     lax.fori_loop(0, gmax + 3, fill_start, (jnp.int32(0), jnp.int32(0)))
 
-    def fill_row(c, carry):
-        who, place = carry
-        count = aggs[grp, who]
-        slot = jnp.where(place < 2, gmax - 4 + place,
-                         jnp.where(place >= count - 2, gmax + place - count, gmax - 2 + place - count))
-        slot_tab[c] = jnp.clip(slot, 0, gmax - 1)
-        who_tab[c] = who
-        done = (place + 1 >= count).astype(jnp.int32)
-        return jnp.minimum(who + done, members - 1), (1 - done) * (place + 1)
-
-    lax.fori_loop(0, coarse, fill_row, (jnp.int32(0), jnp.int32(0)))
+
+    def to_next(r):
+        return pltpu.make_async_remote_copy(
+            src_ref=ghost_out.at[pl.ds(KP * r, KP)], dst_ref=edge.at[pl.ds(STRIDE * r + LEAD, KP)],
+            send_sem=halo_send.at[r], recv_sem=halo_recv.at[r], device_id=next_dev, device_id_type=MESH)
+
+    def to_prev(r):
+        return pltpu.make_async_remote_copy(
+            src_ref=p_hbm.at[pl.ds(KP * r, KP)],
+            dst_ref=edge.at[pl.ds(STRIDE * (5 * HALO + r) + LEAD, KP)],
+            send_sem=halo_send.at[HALO + r], recv_sem=halo_recv.at[HALO + r],
+            device_id=prev_dev, device_id_type=MESH)
+
+    pl.semaphore_wait(barrier, members - 1 + 4)
+    for r in range(HALO):
+        to_prev(r).start()
 
     blank = jnp.zeros((tile, tile), BF16)
 
@@ -113,6 +128,7 @@
     lax.fori_loop(0, 6 * HALO + 1, blank_row(edge), 0)
     pt[cap] = jnp.zeros((KP * tile, tile), BF16)
     a_early[KA * EARLY] = blank
+    a_mid[KA * EARLY] = blank
     a_all[KA * cap] = blank
 
     def blank_band(s, _):
@@ -123,27 +139,12 @@
 
     whole = own.at[pl.ds(0, KP * cap)]
     pltpu.make_async_copy(whole, whole, p_sem).wait()
-
-    def to_next(r):
-        return pltpu.make_async_remote_copy(
-            src_ref=ghost_out.at[pl.ds(KP * r, KP)], dst_ref=edge.at[pl.ds(STRIDE * r + LEAD, KP)],
-            send_sem=halo_send.at[r], recv_sem=halo_recv.at[r], device_id=next_dev, device_id_type=MESH)
-
-    def to_prev(r):
-        return pltpu.make_async_remote_copy(
-            src_ref=own.at[pl.ds(STRIDE * r + LEAD, KP)],
-            dst_ref=edge.at[pl.ds(STRIDE * (5 * HALO + r) + LEAD, KP)],
-            send_sem=halo_send.at[HALO + r], recv_sem=halo_recv.at[HALO + r],
-            device_id=prev_dev, device_id_type=MESH)
-
-    def halo_out():
-        for r in range(HALO):
-            for q in range(KP):
-                ghost_out[KP * r + q] = own[STRIDE * jnp.maximum(n - HALO + r, 0) + LEAD + q]
-        pl.semaphore_wait(barrier, members - 1 + 4)
-        for r in range(HALO):
-            to_next(r).start()
-            to_prev(r).start()
+    for r in range(HALO):
+        for q in range(KP):
+            ghost_out[KP * r + q] = own[STRIDE * jnp.maximum(n - HALO + r, 0) + LEAD + q]
+        to_next(r).start()
+
+    def edge_table():
         for r in range(2 * HALO):
             for q in range(KP):
                 edge[STRIDE * (HALO + r) + LEAD + q] = own[STRIDE * r + LEAD + q]
@@ -252,23 +253,31 @@
         for t in range(0, CHUNK, 2):
             ap_pair(position + t, HALO + position + t, a_ref, a_first, blank_tile, own, inner_index)
 
-    early.wait()
-    lax.fori_loop(0, EARLY // CHUNK, lambda h, _: (quarter(CHUNK * h, a_early, HALO, KA * EARLY), 0)[1], 0)
-    halo_out()
-    aggregate(1)
-    aggregate(2)
-    whole_a.wait()
-
-    def turn(w, _):
-        lax.fori_loop(0, 2, lambda h, _: (quarter(2 * CHUNK * w + CHUNK * h, a_all, 0, KA * cap), 0)[1], 0)
+    def turn(w, a_ref, a_first, blank_tile):
+        lax.fori_loop(
+            0, 2, lambda h, _: (quarter(2 * CHUNK * w + CHUNK * h, a_ref, a_first, blank_tile), 0)[1], 0)
         aggregate(1 + 2 * w)
         aggregate(2 + 2 * w)
+
+    def depart(w):
         for o in range(BAND):
             send[:, (w - 1) * BAND + o] = pack(band[1 + 2 * w, o], band[2 + 2 * w, o])
         send_out((w - 1) * BAND, BAND, w - 1)
-        return 0
-
-    lax.fori_loop(1, inner // (2 * CHUNK), turn, 0)
+
+    early_copy(0, EARLY).wait()
+    turn(0, a_early, HALO, KA * EARLY)
+    mid_copy(0, EARLY).wait()
+    turn(1, a_mid, HALO + EARLY, KA * EARLY)
+    depart(1)
+    edge_table()
+    whole_a.wait()
+
+    def later(w, _):
+        turn(w, a_all, 0, KA * cap)
+        depart(w)
+        return 0
+
+    lax.fori_loop(2, inner // (2 * CHUNK), later, 0)
 
     for r in range(HALO):
         to_next(r).wait_recv()
@@ -304,6 +313,18 @@
         send[:, spill + e] = pack(near[0, e], band[gmax + 1, e] + jnp.where(ga == 1, near[2, e], 0.0))
     send_out(spill, WIDE, pairs)
 
+    def fill_row(c, carry):
+        who, place = carry
+        count = aggs[grp, who]
+        slot = jnp.where(place < 2, gmax - 4 + place,
+                         jnp.where(place >= count - 2, gmax + place - count, gmax - 2 + place - count))
+        slot_tab[c] = jnp.clip(slot, 0, gmax - 1)
+        who_tab[c] = who
+        done = (place + 1 >= count).astype(jnp.int32)
+        return jnp.minimum(who + done, members - 1), (1 - done) * (place + 1)
+
+    lax.fori_loop(0, coarse, fill_row, (jnp.int32(0), jnp.int32(0)))
+
     def arrive(begin, size, index):
         lax.fori_loop(1, members, lambda s, _: (piece(s, begin, size, index).wait_recv(), 0)[1], 0)
         kept(begin, size, index).wait()
@@ -421,12 +442,6 @@
     for r in range(HALO):
         to_next(r).wait_send()
         to_prev(r).wait_send()
-
-
-def write_out(held, out_hbm, sem):
-    copy = pltpu.make_async_copy(held, out_hbm, sem)
-    copy.start()
-    copy.wait()
 
 
 def local(a_tiles, p_tiles, a_offsets, agg_counts, row_counts, flows):
@@ -443,12 +458,13 @@
     smem = pl.BlockSpec(memory_space=pltpu.SMEM)
     hbm = pl.BlockSpec(memory_space=pl.ANY)
     vmem = pl.BlockSpec(memory_space=pltpu.VMEM)
-    held = pl.pallas_call(
+    return pl.pallas_call(
         functools.partial(fused, (groups, members, cap, tile)),
         out_shape=pltpu.VMEM((out_cap, BAND, share, tile), F32),
         in_specs=[hbm, hbm, smem, smem, smem, smem],
         out_specs=vmem,
         scratch_shapes=[
+            pltpu.VMEM((KA * EARLY + 1, tile, tile), BF16),
             pltpu.VMEM((KA * EARLY + 1, tile, tile), BF16),
             pltpu.VMEM((KA * cap + 1, tile, tile), BF16),
             pltpu.VMEM((STRIDE * cap + LEAD, tile, tile), BF16),
@@ -467,7 +483,7 @@
             pltpu.SMEM((cap + 1,), jnp.int32),
             pltpu.SMEM((coarse,), jnp.int32),
             pltpu.SMEM((coarse,), jnp.int32),
-            pltpu.SemaphoreType.DMA((2,)),
+            pltpu.SemaphoreType.DMA((3,)),
             pltpu.SemaphoreType.DMA,
             pltpu.SemaphoreType.DMA((2 * HALO,)),
             pltpu.SemaphoreType.DMA((2 * HALO,)),
@@ -482,14 +498,6 @@
         cost_estimate=pl.CostEstimate(flops=7_500_000_000, bytes_accessed=20_000_000, transcendentals=0),
     )(a_tiles.reshape(cap * KA, tile, tile), p_tiles.reshape(cap * KP, tile, tile), a_offsets.T,
       agg_counts, row_counts, flows.T)
-    return pl.pallas_call(
-        write_out,
-        out_shape=jax.ShapeDtypeStruct((out_cap, BAND, share, tile), F32),
-        in_specs=[vmem],
-        out_specs=hbm,
-        scratch_shapes=[pltpu.SemaphoreType.DMA],
-        cost_estimate=pl.CostEstimate(flops=0, bytes_accessed=6_800_000, transcendentals=0),
-    )(held)
 
 
 def solution(mesh):

time: 69.6 us -> 64.1 us (0.921)
  Pallas kernels: 67.5 us -> 62.2 us
    pallas_call x1 -> x0, Pallas kernels: 3.7 us -> none  [local(): pl.pallas_call(write_out, out_shape=jax.ShapeDtypeStruct((out_cap, BAND,...]
    pallas_call x1, Pallas kernels: 63.8 us -> 62.2 us  [local(): pl.pallas_call(functools.partial(fused, (groups, members, cap, tile)), ou...]
    unnamed x2 -> x1, local copies, waits for them, and re-layouts: 1.69 us -> 1.74 us
where the time goes in v3:
time: 64.1 us; the launch traced here: 64 us
  Pallas kernels  62.2 us (97%)
  local copies, waits for them, and re-layouts  1.74 us (3%)
    pallas_call x1, Pallas kernels, local(): pl.pallas_call(functools.partial(fused, (groups, members, cap, tile)), ou...  62.2 us
    unnamed x1, local copies, waits for them, and re-layouts  1.74 us

profile of v3, /device:TPU:1, one launch (start us, length us, event | category | flops | bytes accessed | tf_op | source)
XLA Modules:
  0.0 64.0 jit_solution(3612765507664519977)
XLA Ops:
  0.0 62.2 %shard_map.64 = f32[118,7,8,128]{3,2,1,0:T(8,128)S(1)} custom-call(bf16[336,128,128]{2,1,0:T(8,128)(2,1)} %bitcast.4, bf16[144,128,128]{2,1,0:T(8,128)(2,1)} %bitcast.5, s32[7,48]{1,0:T(8,128)} %bitcast.6, s32[8,16]{1,0:T(8,128)} %aggs.1, s32[8,16]{1,0:T(8,128)} %rows.1, s32[2,8]{1,0:T(2,128)} %bitcast.7), custom_call_target="tpu_custom_call" | custom-call | flops 7500000256 | bytes 20000000 | tf_op jit(solution)/shard_map/pallas_call | solution.py:461
  62.3 1.7 %copy.8 = f32[118,7,8,128]{3,2,1,0:T(8,128)} copy(f32[118,7,8,128]{3,2,1,0:T(8,128)S(1)} %shard_map.64) | data formatting | bytes 6766592

commit v4 on v3

--- a/solution.py
+++ b/solution.py
@@ -23,7 +23,7 @@
 
 
 def fused(sizes, a_hbm, p_hbm, offs, aggs, rows, flows, outv,
-          a_early, a_mid, a_all, own, edge, ghost_out, ap, pt, band, near, send, recv, foreign, zsend, zrecv,
+          a_early, a_mid, a_all, own, edge, ghost_out, ap, pt, unit, band, near, send, recv, foreign, zsend, zrecv,
           start_tab, agg_tab, slot_tab, who_tab,
           a_sem, p_sem, halo_send, halo_recv, send_sem, recv_sem, self_sem, z_send, z_recv):
     groups, members, cap, tile = sizes
@@ -127,6 +127,8 @@
     lax.fori_loop(0, cap + 1, blank_row(own), 0)
     lax.fori_loop(0, 6 * HALO + 1, blank_row(edge), 0)
     pt[cap] = jnp.zeros((KP * tile, tile), BF16)
+    across, along = (lax.broadcasted_iota(jnp.int32, (tile, tile), axis) for axis in (0, 1))
+    unit[...] = jnp.where(across == along, 1.0, 0.0).astype(BF16)
     a_early[KA * EARLY] = blank
     a_mid[KA * EARLY] = blank
     a_all[KA * cap] = blank
@@ -186,9 +188,11 @@
                 lower.append(out[tile:, e * tile:(e + 1) * tile])
         for e in range(WIDE):
             ap[position + 1, e] = jnp.where(same, lower[e], lower[e + 1]).astype(BF16)
-        for t in (0, 1):
-            for q in range(KP):
-                pt[position + t, pl.ds(q * tile, tile), :] = own[STRIDE * (row + t) + LEAD + q].T
+        mine = [own[STRIDE * (row + t) + LEAD + q] for t in (0, 1) for q in range(KP)]
+        turned = lax.dot_general(
+            unit[...], jnp.concatenate(mine, axis=0), (((1,), (1,)), ((), ())), preferred_element_type=F32)
+        for i in range(2 * KP):
+            pt[position + i // KP, pl.ds(i % KP * tile, tile), :] = turned[:, i * tile:(i + 1) * tile].astype(BF16)
 
     def inner_index(target):
         return jnp.clip(target, 0, cap - 1)
@@ -472,6 +476,7 @@
             pltpu.VMEM((HALO * KP, tile, tile), BF16),
             pltpu.VMEM((cap, WIDE, tile, tile), BF16),
             pltpu.VMEM((cap + 1, KP * tile, tile), BF16),
+            pltpu.VMEM((tile, tile), BF16),
             pltpu.VMEM((gmax + 2, BAND, members, share, tile), F32),
             pltpu.VMEM((KP, WIDE, members, share, tile), F32),
             pltpu.VMEM((members, pieces, 2 * share, tile), BF16),

time: 64.1 us -> 64.1 us (level)
  no operation moved by 1% of the time
where the time goes in v4:
time: 64.1 us; the launch traced here: 64 us
  Pallas kernels  62.2 us (97%)
  local copies, waits for them, and re-layouts  1.74 us (3%)
    pallas_call x1, Pallas kernels, local(): pl.pallas_call(functools.partial(fused, (groups, members, cap, tile)), ou...  62.2 us
    unnamed x1, local copies, waits for them, and re-layouts  1.74 us

profile of v4, /device:TPU:1, one launch (start us, length us, event | category | flops | bytes accessed | tf_op | source)
XLA Modules:
  0.0 64.0 jit_solution(5852113957255902636)
XLA Ops:
  0.0 62.2 %shard_map.64 = f32[118,7,8,128]{3,2,1,0:T(8,128)S(1)} custom-call(bf16[336,128,128]{2,1,0:T(8,128)(2,1)} %bitcast.4, bf16[144,128,128]{2,1,0:T(8,128)(2,1)} %bitcast.5, s32[7,48]{1,0:T(8,128)} %bitcast.6, s32[8,16]{1,0:T(8,128)} %aggs.1, s32[8,16]{1,0:T(8,128)} %rows.1, s32[2,8]{1,0:T(2,128)} %bitcast.7), custom_call_target="tpu_custom_call" | custom-call | flops 7500000256 | bytes 20000000 | tf_op jit(solution)/shard_map/pallas_call | solution.py:465
  62.3 1.7 %copy.8 = f32[118,7,8,128]{3,2,1,0:T(8,128)} copy(f32[118,7,8,128]{3,2,1,0:T(8,128)S(1)} %shard_map.64) | data formatting | bytes 6766592

commit v5 on v3

--- a/solution.py
+++ b/solution.py
@@ -34,8 +34,10 @@
     out_cap = outv.shape[0]
     share = tile // members
     side = 2 if members == 4 else 4
-    spill = pairs * BAND
+    spill = pairs * BAND - 1
     total = spill + WIDE
+    fourth = (pairs - 2) * BAND
+    fifth = fourth + BAND - 1
     inner = cap - 2 * HALO
     grp = lax.axis_index("grp")
     mem = lax.axis_index("mem")
@@ -45,6 +47,16 @@
     next_dev = (lax.rem(grp + last, groups), lax.rem(mem + 1, members))
     prev_dev = (lax.rem(grp + groups - first, groups), lax.rem(mem + members - 1, members))
 
+    barrier = pltpu.get_barrier_semaphore()
+
+    def greet(step, _):
+        pl.semaphore_signal(barrier, inc=1, device_id=(grp, lax.rem(mem + step, members)), device_id_type=MESH)
+        return 0
+
+    lax.fori_loop(1, members, greet, 0)
+    for device in ((up, mem), (down, mem), next_dev, prev_dev):
+        pl.semaphore_signal(barrier, inc=1, device_id=device, device_id_type=MESH)
+
     def p_copy(r):
         return pltpu.make_async_copy(p_hbm.at[pl.ds(KP * r, KP)], own.at[pl.ds(STRIDE * r + LEAD, KP)], p_sem)
 
@@ -61,22 +73,64 @@
 
     whole_a = pltpu.make_async_copy(a_hbm, a_all.at[pl.ds(0, KA * cap)], a_sem.at[1])
     lax.fori_loop(0, cap, lambda r, _: (p_copy(r).start(), 0)[1], 0)
+
+    n = rows[grp, mem]
+    ga = aggs[grp, mem]
+
+
+    def to_next(r):
+        return pltpu.make_async_remote_copy(
+            src_ref=ghost_out.at[pl.ds(KP * r, KP)], dst_ref=edge.at[pl.ds(STRIDE * r + LEAD, KP)],
+            send_sem=halo_send.at[r], recv_sem=halo_recv.at[r], device_id=next_dev, device_id_type=MESH)
+
+    def to_prev(r):
+        return pltpu.make_async_remote_copy(
+            src_ref=p_hbm.at[pl.ds(KP * r, KP)],
+            dst_ref=edge.at[pl.ds(STRIDE * (5 * HALO + r) + LEAD, KP)],
+            send_sem=halo_send.at[HALO + r], recv_sem=halo_recv.at[HALO + r],
+            device_id=prev_dev, device_id_type=MESH)
+
+    pl.semaphore_wait(barrier, members - 1 + 4)
+    for r in range(HALO):
+        to_prev(r).start()
     lax.fori_loop(0, EARLY, lambda r, _: (early_copy(r, 1).start(), 0)[1], 0)
     lax.fori_loop(0, EARLY, lambda r, _: (mid_copy(r, 1).start(), 0)[1], 0)
     lax.fori_loop(0, cap, lambda r, _: (a_copy(r).start(), 0)[1], 0)
 
-    barrier = pltpu.get_barrier_semaphore()
-
-    def greet(step, _):
-        pl.semaphore_signal(barrier, inc=1, device_id=(grp, lax.rem(mem + step, members)), device_id_type=MESH)
-        return 0
-
-    lax.fori_loop(1, members, greet, 0)
-    for device in ((up, mem), (down, mem), next_dev, prev_dev):
-        pl.semaphore_signal(barrier, inc=1, device_id=device, device_id_type=MESH)
-
-    n = rows[grp, mem]
-    ga = aggs[grp, mem]
+    blank = jnp.zeros((tile, tile), BF16)
+
+    def blank_row(table):
+        def body(r, _):
+            for e in range(LEAD):
+                table[STRIDE * r + e] = blank
+            return 0
+        return body
+
+    lax.fori_loop(0, cap + 1, blank_row(own), 0)
+    lax.fori_loop(0, 6 * HALO + 1, blank_row(edge), 0)
+    pt[cap] = jnp.zeros((KP * tile, tile), BF16)
+    a_early[KA * EARLY] = blank
+    a_mid[KA * EARLY] = blank
+    a_all[KA * cap] = blank
+
+    def blank_band(s, _):
+        band[s] = jnp.zeros((BAND, members, share, tile), F32)
+        return 0
+
+    lax.fori_loop(0, gmax + 2, blank_band, 0)
+
+    whole = own.at[pl.ds(0, KP * cap)]
+    pltpu.make_async_copy(whole, whole, p_sem).wait()
+    for r in range(HALO):
+        for q in range(KP):
+            ghost_out[KP * r + q] = own[STRIDE * jnp.maximum(n - HALO + r, 0) + LEAD + q]
+        to_next(r).start()
+
+    def edge_table():
+        for r in range(2 * HALO):
+            for q in range(KP):
+                edge[STRIDE * (HALO + r) + LEAD + q] = own[STRIDE * r + LEAD + q]
+                edge[STRIDE * (3 * HALO + r) + LEAD + q] = own[STRIDE * jnp.maximum(n - 2 * HALO + r, 0) + LEAD + q]
 
     def fill_agg(r, carry):
         agg, rest = carry
@@ -97,58 +151,6 @@
         return q, rest
 
     lax.fori_loop(0, gmax + 3, fill_start, (jnp.int32(0), jnp.int32(0)))
-
-
-    def to_next(r):
-        return pltpu.make_async_remote_copy(
-            src_ref=ghost_out.at[pl.ds(KP * r, KP)], dst_ref=edge.at[pl.ds(STRIDE * r + LEAD, KP)],
-            send_sem=halo_send.at[r], recv_sem=halo_recv.at[r], device_id=next_dev, device_id_type=MESH)
-
-    def to_prev(r):
-        return pltpu.make_async_remote_copy(
-            src_ref=p_hbm.at[pl.ds(KP * r, KP)],
-            dst_ref=edge.at[pl.ds(STRIDE * (5 * HALO + r) + LEAD, KP)],
-            send_sem=halo_send.at[HALO + r], recv_sem=halo_recv.at[HALO + r],
-            device_id=prev_dev, device_id_type=MESH)
-
-    pl.semaphore_wait(barrier, members - 1 + 4)
-    for r in range(HALO):
-        to_prev(r).start()
-
-    blank = jnp.zeros((tile, tile), BF16)
-
-    def blank_row(table):
-        def body(r, _):
-            for e in range(LEAD):
-                table[STRIDE * r + e] = blank
-            return 0
-        return body
-
-    lax.fori_loop(0, cap + 1, blank_row(own), 0)
-    lax.fori_loop(0, 6 * HALO + 1, blank_row(edge), 0)
-    pt[cap] = jnp.zeros((KP * tile, tile), BF16)
-    a_early[KA * EARLY] = blank
-    a_mid[KA * EARLY] = blank
-    a_all[KA * cap] = blank
-
-    def blank_band(s, _):
-        band[s] = jnp.zeros((BAND, members, share, tile), F32)
-        return 0
-
-    lax.fori_loop(0, gmax + 2, blank_band, 0)
-
-    whole = own.at[pl.ds(0, KP * cap)]
-    pltpu.make_async_copy(whole, whole, p_sem).wait()
-    for r in range(HALO):
-        for q in range(KP):
-            ghost_out[KP * r + q] = own[STRIDE * jnp.maximum(n - HALO + r, 0) + LEAD + q]
-        to_next(r).start()
-
-    def edge_table():
-        for r in range(2 * HALO):
-            for q in range(KP):
-                edge[STRIDE * (HALO + r) + LEAD + q] = own[STRIDE * r + LEAD + q]
-                edge[STRIDE * (3 * HALO + r) + LEAD + q] = own[STRIDE * jnp.maximum(n - 2 * HALO + r, 0) + LEAD + q]
 
     def ap_pair(position, row, a_ref, a_first, blank_tile, table, index_of):
         agg = agg_tab[row]
@@ -299,16 +301,20 @@
     products(start_tab[0], start_tab[1], put_near)
     shift = jnp.clip(gmax - ga, 0, gmax - 1) + 1
     for o in range(BAND):
-        upper, lower = band[shift, o], band[shift + 1, o]
-        if 1 <= o <= WIDE:
-            upper = upper + near[1, o - 1]
+        lower = band[shift + 1, o]
         if o < WIDE:
             lower = lower + near[2, o]
-        send[:, (pairs - 2) * BAND + o] = pack(upper, lower)
-    send_out((pairs - 2) * BAND, BAND, pairs - 2)
-    for o in range(BAND):
-        send[:, (pairs - 1) * BAND + o] = pack(band[gmax - 1, o], band[gmax, o])
-    send_out((pairs - 1) * BAND, BAND, pairs - 1)
+        if o == 0:
+            send[:, spill - 1] = pack(band[gmax - 1, BAND - 1], lower)
+            continue
+        upper = band[shift, o]
+        if o <= WIDE:
+            upper = upper + near[1, o - 1]
+        send[:, fourth + o - 1] = pack(upper, lower)
+    send_out(fourth, BAND - 1, pairs - 2)
+    for o in range(BAND - 1):
+        send[:, fifth + o] = pack(band[gmax - 1, o], band[gmax, o])
+    send_out(fifth, BAND, pairs - 1)
     for e in range(WIDE):
         send[:, spill + e] = pack(near[0, e], band[gmax + 1, e] + jnp.where(ga == 1, near[2, e], 0.0))
     send_out(spill, WIDE, pairs)
@@ -341,7 +347,33 @@
 
         return lax.fori_loop(0, members, body, 0)
 
-    lax.fori_loop(0, pairs, unpack, 0)
+    lax.fori_loop(0, pairs - 2, unpack, 0)
+    nothing = jnp.zeros((share, tile), F32)
+    arrive(fourth, BAND - 1, pairs - 2)
+
+    def unpack_fourth(who, _):
+        band[gmax - 4, 0, who] = nothing
+        for o in range(1, BAND):
+            both = recv[who, fourth + o - 1].astype(F32)
+            band[gmax - 4, o, who] = both[:share]
+            band[gmax - 3, o, who] = both[share:]
+        return 0
+
+    lax.fori_loop(0, members, unpack_fourth, 0)
+    arrive(fifth, BAND, pairs - 1)
+
+    def unpack_fifth(who, _):
+        for o in range(BAND - 1):
+            both = recv[who, fifth + o].astype(F32)
+            band[gmax - 2, o, who] = both[:share]
+            band[gmax - 1, o, who] = both[share:]
+        both = recv[who, spill - 1].astype(F32)
+        band[gmax - 2, BAND - 1, who] = both[:share]
+        band[gmax - 1, BAND - 1, who] = nothing
+        band[gmax - 3, 0, who] = both[share:]
+        return 0
+
+    lax.fori_loop(0, members, unpack_fifth, 0)
     arrive(spill, WIDE, pairs)
 
     def unpack_spill(who, _):
@@ -371,22 +403,24 @@
         slot, who = slot_tab[row], who_tab[row]
         return [band[slot, o, who] for o in range(BAND)]
 
-    def z_pack(h, _):
-        for way, base in ((0, coarse - fmax), (1, 0)):
+    def z_pack(way, base):
+        def body(h, _):
             one, two = coarse_row(base + 2 * h), coarse_row(base + 2 * h + 1)
             for o in range(BAND):
                 zsend[way, h * BAND + o] = jnp.concatenate([one[o], two[o]], axis=0).astype(BF16)
-        return 0
-
-    lax.fori_loop(0, (fmax + 1) // 2, z_pack, 0)
+            return 0
+        lax.fori_loop(0, (fmax + 1) // 2, body, 0)
+
     ways = [
         pltpu.make_async_remote_copy(
             src_ref=zsend.at[way], dst_ref=zrecv.at[way], send_sem=z_send.at[way], recv_sem=z_recv.at[way],
             device_id=(group, mem), device_id_type=MESH)
         for way, group in ((0, up), (1, down))
     ]
-    for way in ways:
-        way.start()
+    z_pack(0, coarse - fmax)
+    ways[0].start()
+    z_pack(1, 0)
+    ways[1].start()
 
     take_lower = flows[0, down]
     take_upper = flows[1, up]
@@ -421,23 +455,27 @@
 
     tail = 1 + coarse - 2 * fmax
     gather_all(in_middle, fmax, tail)
-    for way in ways:
-        way.wait()
-
-    def z_unpack(h, _):
-        for way, base in ((0, 0), (1, fmax + 1)):
+
+    def z_unpack(way, base):
+        def body(h, _):
             for o in range(BAND):
                 both = zrecv[way, h * BAND + o].astype(F32)
                 foreign[base + 2 * h, o] = both[:share]
                 foreign[base + 2 * h + 1, o] = both[share:]
-        return 0
-
-    lax.fori_loop(0, (fmax + 1) // 2, z_unpack, 0)
+            return 0
+        lax.fori_loop(0, (fmax + 1) // 2, body, 0)
+
+    for way in ways:
+        way.wait_recv()
+    z_unpack(0, 0)
+    z_unpack(1, fmax + 1)
     for e in range(WIDE):
         foreign[fmax - 1, e + 2] += band[gmax, e + 2, 0]
         foreign[fmax + 1, e] += band[gmax + 1, e, members - 1]
     gather_all(at_end, 0, fmax)
     gather_all(at_end, tail, out_cap)
+    for way in ways:
+        way.wait_send()
     lax.fori_loop(1, members, lambda s, _: (piece(s, 0, total, 0).wait_send(), 0)[1], 0)
     for r in range(HALO):
         to_next(r).wait_send()
@@ -452,7 +490,7 @@
     coarse = members * gmax // 2
     fmax = coarse // 8
     share = tile // members
-    pieces = pairs * BAND + WIDE
+    pieces = pairs * BAND - 1 + WIDE
     out_cap = coarse + 2 * fmax - 2
     handed = (fmax + 1) // 2 * BAND
     smem = pl.BlockSpec(memory_space=pltpu.SMEM)

time: 64.1 us -> 63.2 us (0.986)
  Pallas kernels: 62.2 us -> 61.3 us
    pallas_call x1, Pallas kernels: 62.2 us -> 61.3 us  [local(): pl.pallas_call(functools.partial(fused, (groups, members, cap, tile)), ou...]
where the time goes in v5:
time: 63.2 us; the launch traced here: 63 us
  Pallas kernels  61.3 us (97%)
  local copies, waits for them, and re-layouts  1.74 us (3%)
    pallas_call x1, Pallas kernels, local(): pl.pallas_call(functools.partial(fused, (groups, members, cap, tile)), ou...  61.3 us
    unnamed x1, local copies, waits for them, and re-layouts  1.74 us

profile of v5, /device:TPU:1, one launch (start us, length us, event | category | flops | bytes accessed | tf_op | source)
XLA Modules:
  0.0 63.0 jit_solution(9862323944761082664)
XLA Ops:
  0.0 61.3 %shard_map.64 = f32[118,7,8,128]{3,2,1,0:T(8,128)S(1)} custom-call(bf16[336,128,128]{2,1,0:T(8,128)(2,1)} %bitcast.4, bf16[144,128,128]{2,1,0:T(8,128)(2,1)} %bitcast.5, s32[7,48]{1,0:T(8,128)} %bitcast.6, s32[8,16]{1,0:T(8,128)} %aggs.1, s32[8,16]{1,0:T(8,128)} %rows.1, s32[2,8]{1,0:T(2,128)} %bitcast.7), custom_call_target="tpu_custom_call" | custom-call | flops 7500000256 | bytes 20000000 | tf_op jit(solution)/shard_map/pallas_call | solution.py:499
  61.3 1.7 %copy.8 = f32[118,7,8,128]{3,2,1,0:T(8,128)} copy(f32[118,7,8,128]{3,2,1,0:T(8,128)S(1)} %shard_map.64) | data formatting | bytes 6766592

commit v6 on v5

--- a/solution.py
+++ b/solution.py
@@ -264,22 +264,28 @@
     def depart(w):
         for o in range(BAND):
             send[:, (w - 1) * BAND + o] = pack(band[1 + 2 * w, o], band[2 + 2 * w, o])
-        send_out((w - 1) * BAND, BAND, w - 1)
 
     early_copy(0, EARLY).wait()
     turn(0, a_early, HALO, KA * EARLY)
     mid_copy(0, EARLY).wait()
     turn(1, a_mid, HALO + EARLY, KA * EARLY)
     depart(1)
+    send_out(0, BAND, 0)
     edge_table()
     whole_a.wait()
 
     def later(w, _):
         turn(w, a_all, 0, KA * cap)
         depart(w)
+
+        @pl.when(w == 2)
+        def _():
+            send_out(BAND, BAND, 1)
+
         return 0
 
     lax.fori_loop(2, inner // (2 * CHUNK), later, 0)
+    send_out(2 * BAND, fourth - 2 * BAND, 2)
 
     for r in range(HALO):
         to_next(r).wait_recv()
@@ -311,13 +317,12 @@
         if o <= WIDE:
             upper = upper + near[1, o - 1]
         send[:, fourth + o - 1] = pack(upper, lower)
-    send_out(fourth, BAND - 1, pairs - 2)
+    send_out(fourth, BAND - 1, 3)
     for o in range(BAND - 1):
         send[:, fifth + o] = pack(band[gmax - 1, o], band[gmax, o])
-    send_out(fifth, BAND, pairs - 1)
     for e in range(WIDE):
         send[:, spill + e] = pack(near[0, e], band[gmax + 1, e] + jnp.where(ga == 1, near[2, e], 0.0))
-    send_out(spill, WIDE, pairs)
+    send_out(fifth, BAND + WIDE, 4)
 
     def fill_row(c, carry):
         who, place = carry
@@ -336,8 +341,6 @@
         kept(begin, size, index).wait()
 
     def unpack(u, _):
-        arrive(u * BAND, BAND, u)
-
         def body(who, _):
             for o in range(BAND):
                 both = recv[who, u * BAND + o].astype(F32)
@@ -347,9 +350,14 @@
 
         return lax.fori_loop(0, members, body, 0)
 
-    lax.fori_loop(0, pairs - 2, unpack, 0)
+    arrive(0, BAND, 0)
+    unpack(0, 0)
+    arrive(BAND, BAND, 1)
+    unpack(1, 0)
+    arrive(2 * BAND, fourth - 2 * BAND, 2)
+    lax.fori_loop(2, pairs - 2, unpack, 0)
     nothing = jnp.zeros((share, tile), F32)
-    arrive(fourth, BAND - 1, pairs - 2)
+    arrive(fourth, BAND - 1, 3)
 
     def unpack_fourth(who, _):
         band[gmax - 4, 0, who] = nothing
@@ -360,7 +368,7 @@
         return 0
 
     lax.fori_loop(0, members, unpack_fourth, 0)
-    arrive(fifth, BAND, pairs - 1)
+    arrive(fifth, BAND + WIDE, 4)
 
     def unpack_fifth(who, _):
         for o in range(BAND - 1):
@@ -374,7 +382,6 @@
         return 0
 
     lax.fori_loop(0, members, unpack_fifth, 0)
-    arrive(spill, WIDE, pairs)
 
     def unpack_spill(who, _):
         for e in range(WIDE):
@@ -526,8 +533,8 @@
             pltpu.SemaphoreType.DMA((2 * HALO,)),
             pltpu.SemaphoreType.DMA((2 * HALO,)),
             pltpu.SemaphoreType.DMA((members - 1,)),
-            pltpu.SemaphoreType.DMA((pairs + 1, members - 1)),
-            pltpu.SemaphoreType.DMA((pairs + 1,)),
+            pltpu.SemaphoreType.DMA((5, members - 1)),
+            pltpu.SemaphoreType.DMA((5,)),
             pltpu.SemaphoreType.DMA((2,)),
             pltpu.SemaphoreType.DMA((2,)),
         ],

time: 63.2 us -> 64.6 us (1.022)
  Pallas kernels: 61.3 us -> 62.7 us
    pallas_call x1, Pallas kernels: 61.3 us -> 62.7 us  [local(): pl.pallas_call(functools.partial(fused, (groups, members, cap, tile)), ou...]
where the time goes in v6:
time: 64.6 us; the launch traced here: 64.4 us
  Pallas kernels  62.7 us (97%)
  local copies, waits for them, and re-layouts  1.74 us (3%)
    pallas_call x1, Pallas kernels, local(): pl.pallas_call(functools.partial(fused, (groups, members, cap, tile)), ou...  62.7 us
    unnamed x1, local copies, waits for them, and re-layouts  1.74 us

profile of v6, /device:TPU:1, one launch (start us, length us, event | category | flops | bytes accessed | tf_op | source)
XLA Modules:
  0.0 64.4 jit_solution(13000805914829110757)
XLA Ops:
  0.0 62.7 %shard_map.64 = f32[118,7,8,128]{3,2,1,0:T(8,128)S(1)} custom-call(bf16[336,128,128]{2,1,0:T(8,128)(2,1)} %bitcast.4, bf16[144,128,128]{2,1,0:T(8,128)(2,1)} %bitcast.5, s32[7,48]{1,0:T(8,128)} %bitcast.6, s32[8,16]{1,0:T(8,128)} %aggs.1, s32[8,16]{1,0:T(8,128)} %rows.1, s32[2,8]{1,0:T(2,128)} %bitcast.7), custom_call_target="tpu_custom_call" | custom-call | flops 7500000256 | bytes 20000000 | tf_op jit(solution)/shard_map/pallas_call | solution.py:506
  62.7 1.7 %copy.8 = f32[118,7,8,128]{3,2,1,0:T(8,128)} copy(f32[118,7,8,128]{3,2,1,0:T(8,128)S(1)} %shard_map.64) | data formatting | bytes 6766592
